TPU v7x, 512 devices: a whole 4x4x16 slice. The times are simulated.
512 devices in a mesh: step: 2 (over core), lat: 8 (over y, x_hi), lon: 32 (over x_lo, z).
Axes of the slice: x: 4 (x_hi: 2, x_lo: 2; x = x_hi * 2 + x_lo), y: 4, z: 16, core: 2. Of those that a mesh axis runs over, the one named last changes fastest.
Arguments:
- states: bfloat16 [2, 2, 48, 384, 512], P('step', None, 'lat', 'lon'), may hold values from -6 to 6
- final_cot: bfloat16 [2, 48, 384, 512], P(None, 'lat', 'lon'), may hold values from -6 to 6
- step_cot: bfloat16 [2, 48, 384, 512], P(None, 'lat', 'lon'), may hold values from -6 to 6
- w_qkv: bfloat16 [512, 1536], replicated, may hold values from -0.25 to 0.25
- w_out: bfloat16 [512, 512], replicated, may hold values from -0.25 to 0.25
- land_vec: float32 [512], replicated, may hold values from -6 to 6
- land_sea: int32 [48, 384], replicated, may hold values 0 or 1
- ground_level: int32 [48, 384], replicated, may hold values from 0 to 1
- shift_offsets: int32 [2, 2], replicated, may hold values from 1 to 11, as said below
Outputs:
- gradients: bfloat16 [2, 2, 48, 384, 512], P('step', None, 'lat', 'lon')
Inputs may be any that keep to these rules, and one draw needn't show every extreme that they name: `shift_offsets`: row k holds the shifts of the layer applied to state k: latitude from 1 to 5, longitude from 1 to 11; in each column one of the two rows holds that column's largest value.
All inputs are finite; a program needn't handle non-finite values.
Results may differ from a plain program's by a relative error of at most 0.011.
Values may be sent and summed in bfloat16 or wider, within the bound.
A program may use at most 64 MiB of HBM per device.

v0:
```python
import jax
import jax.numpy as jnp
from jax import lax
from jax.sharding import PartitionSpec as P

HEADS = 8
WLAT = 6
WLON = 12


def shifted(value, axis, by):
    size = lax.axis_size(axis)
    return lax.ppermute(value, axis, [(i, (i + by) % size) for i in range(size)])


def as_sent(value):
    return jax.tree.map(lambda a: a.astype(jnp.bfloat16) if a.dtype == jnp.float32 else a, value)


def passed_along(value, axis, steps):
    count = lax.axis_size(axis)
    leading, last = (max(0, -steps), min(count, count - steps))
    return lax.ppermute(value, axis, [(source, source + steps) for source in range(leading, last)])


def to_windows(tensor):
    levels, height, across = (tensor.shape[0], tensor.shape[1], tensor.shape[2])
    trailing = tuple(tensor.shape[3:])
    shaped = tensor.reshape((levels, height // WLAT, WLAT, across // WLON, WLON) + trailing)
    axes_order = (1, 3, 0, 2, 4) + tuple(range(5, 5 + len(trailing)))
    return jnp.transpose(shaped, axes_order).reshape(
        (height // WLAT * (across // WLON), levels * WLAT * WLON) + trailing
    )


def from_windows(tensor, levels, height, across):
    trailing = tuple(tensor.shape[2:])
    shaped = tensor.reshape((height // WLAT, across // WLON, levels, WLAT, WLON) + trailing)
    axes_order = (2, 0, 3, 1, 4) + tuple(range(5, 5 + len(trailing)))
    return jnp.transpose(shaped, axes_order).reshape((levels, height, across) + trailing)


def window_branch(
    state_field, land_block, ground_block, seam_rows, w_select, w_back, land_vec, head_count
):
    levels, height, across, features = state_field.shape
    head_size = features // HEADS
    lifted = state_field + land_block[None, :, :, None] * land_vec[None, None, None, :]
    average = jnp.mean(lifted, axis=-1, keepdims=True)
    centred = lifted - average
    spread = jnp.mean(centred * centred, axis=-1, keepdims=True)
    normed = (centred * lax.rsqrt(spread + 1e-05)).astype(jnp.bfloat16)
    windows = to_windows(normed)
    level_ids = jnp.arange(levels, dtype=jnp.int32)[:, None, None]
    key_valid = to_windows((level_ids >= ground_block[None]).astype(jnp.float32))
    seam_all = to_windows(jnp.broadcast_to(seam_rows[None, :, None], (levels, height, across)))
    allowed = key_valid[:, None, :] * (seam_all[:, :, None] == seam_all[:, None, :]).astype(
        jnp.float32
    )
    projected = jnp.einsum(
        "wnd,de->wne", windows, w_select, preferred_element_type=jnp.float32
    ).astype(jnp.bfloat16)
    projected = projected.reshape(windows.shape[0], windows.shape[1], 3, head_count, head_size)
    query_heads = projected[:, :, 0]
    key_heads = projected[:, :, 1]
    value_heads = projected[:, :, 2]
    scores = jnp.einsum(
        "wnhe,wmhe->whnm", query_heads, key_heads, preferred_element_type=jnp.float32
    ) * head_size ** (-0.5)
    weights = jnp.exp(scores) * allowed[:, None]
    attention = (weights / jnp.sum(weights, axis=-1, keepdims=True)).astype(jnp.bfloat16)
    mixed = jnp.einsum(
        "whnm,wmhe->wnhe", attention, value_heads, preferred_element_type=jnp.float32
    ).astype(jnp.bfloat16)
    mixed = mixed.reshape(windows.shape[0], windows.shape[1], head_count * head_size)
    branch = jnp.einsum("wnf,fd->wnd", mixed, w_back, preferred_element_type=jnp.float32)
    return from_windows(branch, levels, height, across)


def table_block(table, lat_start, lon_start, height, across):
    extended = jnp.concatenate([table, table[: WLAT - 1]], axis=0)
    extended = jnp.concatenate([extended, extended[:, : WLON - 1]], axis=1)
    return lax.dynamic_slice(extended, (lat_start, lon_start), (height, across))


def head_weights(w_qkv, w_out, head_count):
    features = w_qkv.shape[0]
    head_size = features // HEADS
    w_select = w_qkv.reshape(features, 3, HEADS, head_size)
    w_back = w_out.reshape(HEADS, head_size, features)
    return (
        w_select.reshape(features, 3 * head_count * head_size),
        w_back.reshape(head_count * head_size, features),
    )


def layer_adjoint(paired, shifts, land_sea, ground_level, w_select, w_back, land_vec, head_count):
    shift_lat = shifts[0]
    shift_lon = shifts[1]
    height = paired.shape[2]
    across = paired.shape[3]
    edge_rows = shifted(paired[:, :, : WLAT - 1], "lat", -1)
    rolled = lax.dynamic_slice_in_dim(
        jnp.concatenate([paired, edge_rows], axis=2), shift_lat, height, 2
    )
    edge_cols = shifted(rolled[:, :, :, : WLON - 1], "lon", -1)
    rolled = lax.dynamic_slice_in_dim(
        jnp.concatenate([rolled, edge_cols], axis=3), shift_lon, across, 3
    )
    lat_first = lax.axis_index("lat") * height
    lat_start = lat_first + shift_lat
    lon_start = lax.axis_index("lon") * across + shift_lon
    land_block = table_block(land_sea, lat_start, lon_start, height, across).astype(jnp.float32)
    ground_block = table_block(ground_level, lat_start, lon_start, height, across)
    lat_total = land_sea.shape[0]
    seam_rows = (lat_first + jnp.arange(height, dtype=jnp.int32) >= lat_total - shift_lat).astype(
        jnp.float32
    )

    def branch_of(state_field):
        return window_branch(
            state_field, land_block, ground_block, seam_rows, w_select, w_back, land_vec, head_count
        )

    _, pullback = jax.vjp(branch_of, rolled[0].astype(jnp.float32))
    gradient = pullback(rolled[1].astype(jnp.float32))[0]
    edge_cols = shifted(
        gradient[:, :, across - (WLON - 1) :].astype(jnp.bfloat16), "lon", 1
    ).astype(jnp.float32)
    gradient = lax.dynamic_slice_in_dim(
        jnp.concatenate([edge_cols, gradient], axis=2), WLON - 1 - shift_lon, across, 2
    )
    edge_rows = shifted(as_sent(gradient[:, height - (WLAT - 1) :]), "lat", 1)
    gradient = lax.dynamic_slice_in_dim(
        jnp.concatenate([edge_rows, gradient], axis=1), WLAT - 1 - shift_lat, height, 1
    )
    return gradient


def per_device(
    states, final_cot, step_cot, w_qkv, w_out, land_vec, land_sea, ground_level, shift_offsets
):
    step_index = lax.axis_index("step")
    own_state = states[0]
    w_select, w_back = head_weights(w_qkv, w_out, HEADS)
    late_part = layer_adjoint(
        jnp.stack([own_state, final_cot]),
        shift_offsets[1],
        land_sea,
        ground_level,
        w_select,
        w_back,
        land_vec,
        HEADS,
    )
    later_grad = (step_cot.astype(jnp.float32) + final_cot.astype(jnp.float32) + late_part).astype(
        jnp.bfloat16
    )
    arrived = passed_along(later_grad, "step", -1)
    early_part = layer_adjoint(
        jnp.stack([own_state, arrived]),
        shift_offsets[0],
        land_sea,
        ground_level,
        w_select,
        w_back,
        land_vec,
        HEADS,
    )
    earliest = (arrived.astype(jnp.float32) + early_part).astype(jnp.bfloat16)
    result = jnp.where(step_index == 0, earliest, later_grad)
    return result[None]


def solution(mesh):
    return jax.shard_map(
        per_device,
        mesh=mesh,
        in_specs=(
            P("step", None, "lat", "lon", None),
            P(None, "lat", "lon", None),
            P(None, "lat", "lon", None),
            P(),
            P(),
            P(),
            P(),
            P(),
            P(),
        ),
        out_specs=P("step", None, "lat", "lon", None),
        check_vma=False,
    )
```

profile of v0, /device:TPU:2, one launch (start us, length us, event | category | flops | bytes accessed | tf_op | source)
XLA Modules:
  0.0 154.6 jit_solution(12189738824183673344)
XLA Ops:
  0.0 1.1 copy.35
  1.1 0.9 copy.65
  2.1 6.5 %collective-permute-start = (bf16[2,2,5,12,512]{4,3,2,1,0:T(8,128)(2,1)S(1)}, bf16[2,2,5,12,512]{4,3,2,1,0:T(8,128)(2,1)}, u32[]{:S(2)}, u32[]{:S(2)}) collective-permute-start(bf16[2,2,5,12,512]{4,3,2,1,0:T(8,128)(2,1)S(1)} %pad_maximum_fusion.1), channel_id=1, source_target_pairs={{0,224},{32,0},{64,32},{96,64},{128,96},{160,128},{192,160},{224,1... | collective-permute-start | bytes 737288 | tf_op jit(solution)/shard_map/ppermute | solution.py:13
  8.6 0.6 fusion.59
  11.7 0.7 dynamic-slice_convert_fusion
  14.7 0.8 collective-permute-done
  15.5 1.1 fusion.37
  16.6 12.3 %collective-permute-start.1 = (bf16[2,2,6,11,512]{4,3,2,1,0:T(8,128)(2,1)S(1)}, bf16[2,2,6,11,512]{4,3,2,1,0:T(8,128)(2,1)}, u32[]{:S(2)}, u32[]{:S(2)}) collective-permute-start(bf16[2,2,6,11,512]{4,3,2,1,0:T(8,128)(2,1)S(1)} %bitcast.145), channel_id=1, source_target_pairs={{0,31},{1,0},{2,1},{3,2},{4,3},{5,4},{6,5},{7,6},{8,7},{9,8},{10,9... | collective-permute-start | bytes 811016 | tf_op jit(solution)/shard_map/ppermute | solution.py:13
  31.2 0.8 compare_select_fusion.1
  31.9 4.4 %collective-permute-done.1 = bf16[2,2,6,11,512]{4,3,2,1,0:T(8,128)(2,1)} collective-permute-done((bf16[2,2,6,11,512]{4,3,2,1,0:T(8,128)(2,1)S(1)}, bf16[2,2,6,11,512]{4,3,2,1,0:T(8,128)(2,1)}, u32[]{:S(2)}, u32[]{:S(2)}) %collective-permute-start.1) | collective-permute-done | bytes 270368 | tf_op jit(solution)/shard_map/ppermute | solution.py:13
  36.4 1.4 fusion.25
  38.2 0.7 fusion.57
  39.0 0.5 copy-done.24
  39.6 0.7 copy-done.3
  40.3 1.2 convolution_convert_fusion.1
  41.6 1.3 copy.60
  42.9 1.7 %reshape.563 = bf16[144,512]{1,0:T(8,128)(2,1)} reshape(bf16[1,2,6,12,512]{4,3,2,1,0:T(8,128)(2,1)} %get-tuple-element.7) | data formatting | bytes 294912 | tf_op jit(solution)/shard_map/reshape.5
  44.5 2.1 %convolution_convert_fusion.13 = bf16[144,512]{1,0:T(8,128)(2,1)} fusion(bf16[144,512]{1,0:T(8,128)(2,1)} %reshape.563, bf16[512,512]{1,0:T(8,128)(2,1)} %param.13), kind=kOutput, calls=%fused_computation.43 | convolution fusion | flops 75571200 | bytes 819200 | tf_op jit(solution)/shard_map/transpose(jvp(wnf,fd->wnd))/dot_general | solution.py:76
  46.6 1.8 %reshape.564 = bf16[1,144,8,64]{3,2,1,0:T(8,128)(2,1)} reshape(bf16[144,512]{1,0:T(8,128)(2,1)} %convolution_convert_fusion.13) | data formatting | bytes 294912 | tf_op jit(solution)/shard_map/transpose(jvp())/reshape | solution.py:75
  48.5 1.9 %copy.38 = bf16[8,64,144]{2,1,0:T(8,128)(2,1)} copy(bf16[8,64,144]{1,0,2:T(8,128)(2,1)} %bitcast.146) | data formatting | bytes 294912 | tf_op jit(solution)/shard_map/reshape.19
  50.4 0.5 multiply_reduce_fusion.1
  50.9 0.5 copy-done.9
  51.7 0.4 fusion.7
  52.1 0.4 fusion.16
  52.6 0.4 fusion.17
  53.2 1.4 fusion.21
  54.6 1.1 reshape.582
  55.9 1.3 fusion.50
  57.2 0.7 reduce_sum.120
  57.8 0.7 multiply_multiply_fusion.3
  58.5 1.2 fusion.42
  59.8 0.9 fusion.26
  60.8 1.9 %collective-permute-start.2 = (bf16[2,6,11,512]{3,2,1,0:T(8,128)(2,1)S(1)}, bf16[2,6,11,512]{3,2,1,0:T(8,128)(2,1)S(1)}, u32[]{:S(2)}, u32[]{:S(2)}) collective-permute-start(bf16[2,6,11,512]{3,2,1,0:T(8,128)(2,1)S(1)} %slice.169), channel_id=1, source_target_pairs={{0,1},{1,2},{2,3},{3,4},{4,5},{5,6},{6,7},{7,8},{8,9},{9,10},{10,1... | collective-permute-start | bytes 405512 | tf_op jit(solution)/shard_map/ppermute | solution.py:13
  64.0 7.0 %collective-permute-done.2 = bf16[2,6,11,512]{3,2,1,0:T(8,128)(2,1)S(1)} collective-permute-done((bf16[2,6,11,512]{3,2,1,0:T(8,128)(2,1)S(1)}, bf16[2,6,11,512]{3,2,1,0:T(8,128)(2,1)S(1)}, u32[]{:S(2)}, u32[]{:S(2)}) %collective-permute-start.2) | collective-permute-done | bytes 135200 | tf_op jit(solution)/shard_map/ppermute | solution.py:13
  71.2 3.8 %collective-permute-start.3 = (bf16[2,5,12,512]{3,2,1,0:T(8,128)(2,1)S(1)}, bf16[2,5,12,512]{3,2,1,0:T(8,128)(2,1)S(1)}, u32[]{:S(2)}, u32[]{:S(2)}) collective-permute-start(bf16[2,5,12,512]{3,2,1,0:T(8,128)(2,1)S(1)} %slice.171), channel_id=1, source_target_pairs={{0,32},{32,64},{64,96},{96,128},{128,160},{160,192},{192,224},{224... | collective-permute-start | bytes 368648 | tf_op jit(solution)/shard_map/ppermute | solution.py:13
  76.2 5.9 %collective-permute-done.3 = bf16[2,5,12,512]{3,2,1,0:T(8,128)(2,1)S(1)} collective-permute-done((bf16[2,5,12,512]{3,2,1,0:T(8,128)(2,1)S(1)}, bf16[2,5,12,512]{3,2,1,0:T(8,128)(2,1)S(1)}, u32[]{:S(2)}, u32[]{:S(2)}) %collective-permute-start.3) | collective-permute-done | bytes 122912 | tf_op jit(solution)/shard_map/ppermute | solution.py:13
  82.1 1.0 fusion.35
  83.2 1.3 collective-permute-start.4
  84.5 2.0 %collective-permute-done.4 = bf16[2,6,12,512]{3,2,1,0:T(8,128)(2,1)S(1)} collective-permute-done((bf16[2,6,12,512]{3,2,1,0:T(8,128)(2,1)S(1)}, bf16[2,6,12,512]{3,2,1,0:T(8,128)(2,1)S(1)}, u32[]{:S(2)}, u32[]{:S(2)}) %collective-permute-start.4) | collective-permute-done | bytes 147488 | tf_op jit(solution)/shard_map/ppermute | solution.py:23
  86.6 5.4 %collective-permute-start.5 = (bf16[2,2,5,12,512]{4,3,2,1,0:T(8,128)(2,1)S(1)}, bf16[2,2,5,12,512]{4,3,2,1,0:T(8,128)(2,1)S(1)}, u32[]{:S(2)}, u32[]{:S(2)}) collective-permute-start(bf16[2,2,5,12,512]{4,3,2,1,0:T(8,128)(2,1)S(1)} %pad_maximum_fusion), channel_id=1, source_target_pairs={{0,224},{32,0},{64,32},{96,64},{128,96},{160,128},{192,160},{224,1... | collective-permute-start | bytes 737288 | tf_op jit(solution)/shard_map/ppermute | solution.py:13
  94.5 5.2 %collective-permute-done.5 = bf16[2,2,5,12,512]{4,3,2,1,0:T(8,128)(2,1)S(1)} collective-permute-done((bf16[2,2,5,12,512]{4,3,2,1,0:T(8,128)(2,1)S(1)}, bf16[2,2,5,12,512]{4,3,2,1,0:T(8,128)(2,1)S(1)}, u32[]{:S(2)}, u32[]{:S(2)}) %collective-permute-start.5) | collective-permute-done | bytes 245792 | tf_op jit(solution)/shard_map/ppermute | solution.py:13
  99.9 4.7 %collective-permute-start.6 = (bf16[2,2,6,11,512]{4,3,2,1,0:T(8,128)(2,1)S(1)}, bf16[2,2,6,11,512]{4,3,2,1,0:T(8,128)(2,1)}, u32[]{:S(2)}, u32[]{:S(2)}) collective-permute-start(bf16[2,2,6,11,512]{4,3,2,1,0:T(8,128)(2,1)S(1)} %bitcast.144), channel_id=1, source_target_pairs={{0,31},{1,0},{2,1},{3,2},{4,3},{5,4},{6,5},{7,6},{8,7},{9,8},{10,9... | collective-permute-start | bytes 811016 | tf_op jit(solution)/shard_map/ppermute | solution.py:13
  106.7 0.8 compare_select_fusion
  107.4 4.8 %collective-permute-done.6 = bf16[2,2,6,11,512]{4,3,2,1,0:T(8,128)(2,1)} collective-permute-done((bf16[2,2,6,11,512]{4,3,2,1,0:T(8,128)(2,1)S(1)}, bf16[2,2,6,11,512]{4,3,2,1,0:T(8,128)(2,1)}, u32[]{:S(2)}, u32[]{:S(2)}) %collective-permute-start.6) | collective-permute-done | bytes 270368 | tf_op jit(solution)/shard_map/ppermute | solution.py:13
  112.2 1.4 fusion.23
  113.6 0.7 fusion.56
  115.4 0.6 copy-done.22
  116.0 1.2 convolution_convert_fusion
  117.2 1.3 copy.61
  118.5 1.6 %reshape.571 = bf16[144,512]{1,0:T(8,128)(2,1)} reshape(bf16[1,2,6,12,512]{4,3,2,1,0:T(8,128)(2,1)} %get-tuple-element.5) | data formatting | bytes 294912 | tf_op jit(solution)/shard_map/reshape.70
  120.1 2.1 %convolution_convert_fusion.11 = bf16[144,512]{1,0:T(8,128)(2,1)} fusion(bf16[144,512]{1,0:T(8,128)(2,1)} %reshape.571, bf16[512,512]{1,0:T(8,128)(2,1)} %param.13), kind=kOutput, calls=%fused_computation.40 | convolution fusion | flops 75571200 | bytes 819200 | tf_op jit(solution)/shard_map/transpose(jvp(wnf,fd->wnd))/dot_general | solution.py:76
  122.2 1.8 %reshape.572 = bf16[1,144,8,64]{3,2,1,0:T(8,128)(2,1)} reshape(bf16[144,512]{1,0:T(8,128)(2,1)} %convolution_convert_fusion.11) | data formatting | bytes 294912 | tf_op jit(solution)/shard_map/transpose(jvp())/reshape | solution.py:75
  124.1 1.9 %copy.47 = bf16[8,64,144]{2,1,0:T(8,128)(2,1)} copy(bf16[8,64,144]{1,0,2:T(8,128)(2,1)} %bitcast.147) | data formatting | bytes 294912 | tf_op jit(solution)/shard_map/reshape.84
  126.0 1.4 multiply_reduce_fusion
  127.8 0.4 fusion.13
  128.2 0.4 fusion.18
  129.3 0.7 fusion.20
  130.2 0.6 fusion.51
  131.3 0.9 fusion.27
  132.2 1.9 %collective-permute-start.7 = (bf16[2,6,11,512]{3,2,1,0:T(8,128)(2,1)S(1)}, bf16[2,6,11,512]{3,2,1,0:T(8,128)(2,1)S(1)}, u32[]{:S(2)}, u32[]{:S(2)}) collective-permute-start(bf16[2,6,11,512]{3,2,1,0:T(8,128)(2,1)S(1)} %slice.168), channel_id=1, source_target_pairs={{0,1},{1,2},{2,3},{3,4},{4,5},{5,6},{6,7},{7,8},{8,9},{9,10},{10,1... | collective-permute-start | bytes 405512 | tf_op jit(solution)/shard_map/ppermute | solution.py:13
  135.3 7.2 %collective-permute-done.7 = bf16[2,6,11,512]{3,2,1,0:T(8,128)(2,1)S(1)} collective-permute-done((bf16[2,6,11,512]{3,2,1,0:T(8,128)(2,1)S(1)}, bf16[2,6,11,512]{3,2,1,0:T(8,128)(2,1)S(1)}, u32[]{:S(2)}, u32[]{:S(2)}) %collective-permute-start.7) | collective-permute-done | bytes 135200 | tf_op jit(solution)/shard_map/ppermute | solution.py:13
  142.7 2.0 %collective-permute-start.8 = (bf16[2,5,12,512]{3,2,1,0:T(8,128)(2,1)S(1)}, bf16[2,5,12,512]{3,2,1,0:T(8,128)(2,1)S(1)}, u32[]{:S(2)}, u32[]{:S(2)}) collective-permute-start(bf16[2,5,12,512]{3,2,1,0:T(8,128)(2,1)S(1)} %slice.170), channel_id=1, source_target_pairs={{0,32},{32,64},{64,96},{96,128},{128,160},{160,192},{192,224},{224... | collective-permute-start | bytes 368648 | tf_op jit(solution)/shard_map/ppermute | solution.py:13
  146.1 7.5 %collective-permute-done.8 = bf16[2,5,12,512]{3,2,1,0:T(8,128)(2,1)S(1)} collective-permute-done((bf16[2,5,12,512]{3,2,1,0:T(8,128)(2,1)S(1)}, bf16[2,5,12,512]{3,2,1,0:T(8,128)(2,1)S(1)}, u32[]{:S(2)}, u32[]{:S(2)}) %collective-permute-start.8) | collective-permute-done | bytes 122912 | tf_op jit(solution)/shard_map/ppermute | solution.py:13
  153.8 0.8 copy.53
  (124 shorter events, 5.8 us)
Async XLA Ops:
  0.0 40.3 %copy-start = (bf16[512,1536]{1,0:T(8,128)(2,1)S(1)}, bf16[512,1536]{1,0:T(8,128)(2,1)}, u32[]{:S(2)}) copy-start(bf16[512,1536]{1,0:T(8,128)(2,1)} %param.12) | copy-start | bytes 4718596
  0.0 8.6 %copy-start.27 = (s32[2,2]{1,0:T(2,128)S(1)}, s32[2,2]{1,0:T(2,128)}, u32[]{:S(2)}) copy-start(s32[2,2]{1,0:T(2,128)} %param.17) | copy-start | bytes 52
  0.0 11.6 %copy-start.14 = (s32[48,384]{1,0:T(8,128)S(1)}, s32[48,384]{1,0:T(8,128)}, u32[]{:S(2)}) copy-start(s32[48,384]{1,0:T(8,128)} %param.16) | copy-start | bytes 221188
  0.0 11.6 %copy-start.15 = (s32[48,384]{1,0:T(8,128)S(1)}, s32[48,384]{1,0:T(8,128)}, u32[]{:S(2)}) copy-start(s32[48,384]{1,0:T(8,128)} %param.15) | copy-start | bytes 221188
  0.0 14.6 %copy-start.28 = (f32[512]{0:T(512)S(1)}, f32[512]{0:T(512)}, u32[]{:S(2)}) copy-start(f32[512]{0:T(512)} %param.14) | copy-start | bytes 6148
  2.1 13.4 %collective-permute-start = (bf16[2,2,5,12,512]{4,3,2,1,0:T(8,128)(2,1)S(1)}, bf16[2,2,5,12,512]{4,3,2,1,0:T(8,128)(2,1)}, u32[]{:S(2)}, u32[]{:S(2)}) collective-permute-start(bf16[2,2,5,12,512]{4,3,2,1,0:T(8,128)(2,1)S(1)} %pad_maximum_fusion.1), channel_id=1, source_target_pairs={{0,224},{32,0},{64,32},{96,64},{128,96},{160,128},{192,160},{224,1... | collective-permute-start | bytes 737288 | tf_op jit(solution)/shard_map/ppermute | solution.py:13
  16.6 19.8 %collective-permute-start.1 = (bf16[2,2,6,11,512]{4,3,2,1,0:T(8,128)(2,1)S(1)}, bf16[2,2,6,11,512]{4,3,2,1,0:T(8,128)(2,1)}, u32[]{:S(2)}, u32[]{:S(2)}) collective-permute-start(bf16[2,2,6,11,512]{4,3,2,1,0:T(8,128)(2,1)S(1)} %bitcast.145), channel_id=1, source_target_pairs={{0,31},{1,0},{2,1},{3,2},{4,3},{5,4},{6,5},{7,6},{8,7},{9,8},{10,9... | collective-permute-start | bytes 811016 | tf_op jit(solution)/shard_map/ppermute | solution.py:13
  30.3 9.3 %copy-start.1 = (f32[144,512]{1,0:T(8,128)}, f32[144,512]{1,0:T(8,128)S(1)}, u32[]{:S(2)}) copy-start(f32[144,512]{1,0:T(8,128)S(1)} %add.162) | copy-start | bytes 884740
  38.1 1.0 copy-start.16
  38.2 3.4 %copy-start.18 = (f32[144]{0:T(256)}, f32[144]{0:T(256)S(1)}, u32[]{:S(2)}) copy-start(f32[144]{0:T(256)S(1)} %div.103) | copy-start | bytes 1732
  39.0 0.6 copy-start.24
  39.6 2.0 %copy-start.21 = (f32[144]{0:T(256)}, f32[144]{0:T(256)S(1)}, u32[]{:S(2)}) copy-start(f32[144]{0:T(256)S(1)} %rsqrt.28) | copy-start | bytes 1732
  39.6 0.7 copy-start.3
  42.9 7.5 %copy-start.7 = (f32[144,144]{0,1:T(8,128)S(1)}, f32[144,144]{0,1:T(8,128)}, u32[]{:S(2)}) copy-start(f32[144,144]{0,1:T(8,128)} %compare_select_fusion.1) | copy-start | bytes 248836
  50.4 0.9 copy-start.9
  54.6 3.9 %copy-start.2 = (f32[144,512]{1,0:T(8,128)S(1)}, f32[144,512]{1,0:T(8,128)}, u32[]{:S(2)}) copy-start(f32[144,512]{1,0:T(8,128)} %copy-done.1) | copy-start | bytes 884740
  54.6 3.9 %copy-start.4 = (f32[144,512]{1,0:T(8,128)S(1)}, f32[144,512]{1,0:T(8,128)}, u32[]{:S(2)}) copy-start(f32[144,512]{1,0:T(8,128)} %copy-done.3) | copy-start | bytes 884740
  60.8 10.2 %collective-permute-start.2 = (bf16[2,6,11,512]{3,2,1,0:T(8,128)(2,1)S(1)}, bf16[2,6,11,512]{3,2,1,0:T(8,128)(2,1)S(1)}, u32[]{:S(2)}, u32[]{:S(2)}) collective-permute-start(bf16[2,6,11,512]{3,2,1,0:T(8,128)(2,1)S(1)} %slice.169), channel_id=1, source_target_pairs={{0,1},{1,2},{2,3},{3,4},{4,5},{5,6},{6,7},{7,8},{8,9},{9,10},{10,1... | collective-permute-start | bytes 405512 | tf_op jit(solution)/shard_map/ppermute | solution.py:13
  64.0 18.1 %copy-start.13 = (bf16[2,6,12,512]{3,0,2,1:T(2,128)(2,1)S(1)}, bf16[2,6,12,512]{3,0,2,1:T(2,128)(2,1)}, u32[]{:S(2)}) copy-start(bf16[2,6,12,512]{3,0,2,1:T(2,128)(2,1)} %param.10) | copy-start | bytes 442372
  71.2 10.8 %collective-permute-start.3 = (bf16[2,5,12,512]{3,2,1,0:T(8,128)(2,1)S(1)}, bf16[2,5,12,512]{3,2,1,0:T(8,128)(2,1)S(1)}, u32[]{:S(2)}, u32[]{:S(2)}) collective-permute-start(bf16[2,5,12,512]{3,2,1,0:T(8,128)(2,1)S(1)} %slice.171), channel_id=1, source_target_pairs={{0,32},{32,64},{64,96},{96,128},{128,160},{160,192},{192,224},{224... | collective-permute-start | bytes 368648 | tf_op jit(solution)/shard_map/ppermute | solution.py:13
  76.2 18.3 %copy-start.17 = (s32[6,12]{1,0:T(8,128)S(1)}, s32[6,12]{1,0:T(8,128)}, u32[]{:S(2)}) copy-start(s32[6,12]{1,0:T(8,128)} %get-tuple-element.32) | copy-start | bytes 868
  83.2 22.6 %copy-start.11 = (bf16[2,6,12,512]{3,2,1,0:T(8,128)(2,1)}, bf16[2,6,12,512]{3,2,1,0:T(8,128)(2,1)S(1)}, u32[]{:S(2)}) copy-start(bf16[2,6,12,512]{3,2,1,0:T(8,128)(2,1)S(1)} %fusion.35) | copy-start | bytes 442372
  83.2 3.3 %collective-permute-start.4 = (bf16[2,6,12,512]{3,2,1,0:T(8,128)(2,1)S(1)}, bf16[2,6,12,512]{3,2,1,0:T(8,128)(2,1)S(1)}, u32[]{:S(2)}, u32[]{:S(2)}) collective-permute-start(bf16[2,6,12,512]{3,2,1,0:T(8,128)(2,1)S(1)} %fusion.35), channel_id=1, source_target_pairs={{256,0},{257,1},{258,2},{259,3},{260,4},{261,5},{262,6},{263,7},{2... | collective-permute-start | bytes 442376 | tf_op jit(solution)/shard_map/ppermute | solution.py:23
  86.5 19.3 %copy-start.5 = (bf16[2,6,12,512]{3,2,1,0:T(8,128)(2,1)}, bf16[2,6,12,512]{3,2,1,0:T(8,128)(2,1)S(1)}, u32[]{:S(2)}) copy-start(bf16[2,6,12,512]{3,2,1,0:T(8,128)(2,1)S(1)} %collective-permute-done.4) | copy-start | bytes 442372
  86.6 13.2 %collective-permute-start.5 = (bf16[2,2,5,12,512]{4,3,2,1,0:T(8,128)(2,1)S(1)}, bf16[2,2,5,12,512]{4,3,2,1,0:T(8,128)(2,1)S(1)}, u32[]{:S(2)}, u32[]{:S(2)}) collective-permute-start(bf16[2,2,5,12,512]{4,3,2,1,0:T(8,128)(2,1)S(1)} %pad_maximum_fusion), channel_id=1, source_target_pairs={{0,224},{32,0},{64,32},{96,64},{128,96},{160,128},{192,160},{224,1... | collective-permute-start | bytes 737288 | tf_op jit(solution)/shard_map/ppermute | solution.py:13
  99.9 12.3 %collective-permute-start.6 = (bf16[2,2,6,11,512]{4,3,2,1,0:T(8,128)(2,1)S(1)}, bf16[2,2,6,11,512]{4,3,2,1,0:T(8,128)(2,1)}, u32[]{:S(2)}, u32[]{:S(2)}) collective-permute-start(bf16[2,2,6,11,512]{4,3,2,1,0:T(8,128)(2,1)S(1)} %bitcast.144), channel_id=1, source_target_pairs={{0,31},{1,0},{2,1},{3,2},{4,3},{5,4},{6,5},{7,6},{8,7},{9,8},{10,9... | collective-permute-start | bytes 811016 | tf_op jit(solution)/shard_map/ppermute | solution.py:13
  114.7 0.6 copy-start.19
  114.9 0.5 copy-start.25
  115.4 0.6 copy-start.22
  126.0 1.5 copy-start.8
  126.0 1.5 copy-start.10
  129.9 1.0 copy-start.26
  130.0 1.0 copy-start.20
  130.0 1.0 copy-start.23
  132.2 10.3 %collective-permute-start.7 = (bf16[2,6,11,512]{3,2,1,0:T(8,128)(2,1)S(1)}, bf16[2,6,11,512]{3,2,1,0:T(8,128)(2,1)S(1)}, u32[]{:S(2)}, u32[]{:S(2)}) collective-permute-start(bf16[2,6,11,512]{3,2,1,0:T(8,128)(2,1)S(1)} %slice.168), channel_id=1, source_target_pairs={{0,1},{1,2},{2,3},{3,4},{4,5},{5,6},{6,7},{7,8},{8,9},{9,10},{10,1... | collective-permute-start | bytes 405512 | tf_op jit(solution)/shard_map/ppermute | solution.py:13
  135.3 18.3 %copy-start.6 = (bf16[2,6,12,512]{3,2,1,0:T(8,128)(2,1)S(1)}, bf16[2,6,12,512]{3,2,1,0:T(8,128)(2,1)}, u32[]{:S(2)}) copy-start(bf16[2,6,12,512]{3,2,1,0:T(8,128)(2,1)} %copy-done.5) | copy-start | bytes 442372
  135.3 18.3 %copy-start.12 = (bf16[2,6,12,512]{3,2,1,0:T(8,128)(2,1)S(1)}, bf16[2,6,12,512]{3,2,1,0:T(8,128)(2,1)}, u32[]{:S(2)}) copy-start(bf16[2,6,12,512]{3,2,1,0:T(8,128)(2,1)} %copy-done.11) | copy-start | bytes 442372
  142.7 10.8 %collective-permute-start.8 = (bf16[2,5,12,512]{3,2,1,0:T(8,128)(2,1)S(1)}, bf16[2,5,12,512]{3,2,1,0:T(8,128)(2,1)S(1)}, u32[]{:S(2)}, u32[]{:S(2)}) collective-permute-start(bf16[2,5,12,512]{3,2,1,0:T(8,128)(2,1)S(1)} %slice.170), channel_id=1, source_target_pairs={{0,32},{32,64},{64,96},{96,128},{128,160},{160,192},{192,224},{224... | collective-permute-start | bytes 368648 | tf_op jit(solution)/shard_map/ppermute | solution.py:13
where the time goes:
time: 156 us; the launch traced here: 155 us
  waiting for transfers between devices  44.9 us (29%)
  starting transfers between devices  39.9 us (26%)
  local copies, waits for them, and re-layouts  22.8 us (15%)
  other arithmetic  16.8 us (11%)
  between operations  16.3 us (10%)
  matrix products  13.9 us (9%)
    ppermute x8, waiting for transfers between devices, shifted(): lax.ppermute(value, axis, [(i, (i + by) % size) for i in range(size)])  42.9 us
    ppermute x8, starting transfers between devices, shifted(): lax.ppermute(value, axis, [(i, (i + by) % size) for i in range(size)])  38.6 us
    another operation x4, local copies, waits for them, and re-layouts  7.07 us
    unnamed x60, local copies, waits for them, and re-layouts  4.91 us
    dot_general x4, matrix products, window_branch(): jnp.einsum('wnd,de->wne', windows, w_select, preferred_element_type=jnp.f...  4.53 us
    dot_general x2, matrix products, window_branch(): jnp.einsum('wnf,fd->wnd', mixed, w_back, preferred_element_type=jnp.float32)  4.21 us
    reshape x2, local copies, waits for them, and re-layouts, window_branch(): mixed.reshape(windows.shape[0], windows.shape[1], head_count * head_size)  3.67 us
    dot_general x6, matrix products, window_branch(): jnp.einsum('wnhe,wmhe->whnm', query_heads, key_heads, preferred_element_t...  3.61 us
  transfers between devices with their start and end apart: 9, of which 9 were waited for; matrix products, arithmetic and copies ran while one was open for 2% of the time, Pallas kernels for 0%

commit v1 on v0

v1 whole, which is shorter than its diff:
```python
import functools

import jax
import jax.numpy as jnp
import numpy as np
from jax import lax
from jax.experimental import pallas as pl
from jax.experimental.pallas import tpu as pltpu
from jax.sharding import PartitionSpec as P

HEADS = 8
LEV = 2
WLAT = 6
WLON = 12
TOK = WLAT * WLON * LEV
MESH = pl.DeviceIdType.MESH
F32 = jnp.float32
BF16 = jnp.bfloat16
NT = (((1,), (1,)), ((), ()))
TN = (((0,), (0,)), ((), ()))


def up_to(value, unit):
    return -(-value // unit) * unit


class Exchange:
    def __init__(self, first_rows, last_rows, first_cols, last_cols):
        rows = {-1: range(first_rows), 0: range(WLAT), 1: range(WLAT - last_rows, WLAT)}
        cols = {-1: range(first_cols), 0: range(WLON), 1: range(WLON - last_cols, WLON)}
        self.pieces = []
        pack, codes = [], list(range(4 * TOK, 5 * TOK))
        offset = 0
        for dy, dx in ((1, 0), (-1, 0), (0, 1), (0, -1), (1, 1), (1, -1), (-1, 1), (-1, -1)):
            tokens = [(r * WLON + c) * LEV + l for r in rows[dy] for c in cols[dx] for l in range(LEV)]
            if not tokens:
                continue
            size = up_to(len(tokens), 16)
            zone = (1 - dy) * 3 + 1 - dx
            filler = [-1] * (size - len(tokens))
            codes += [zone * TOK + token for token in tokens] + filler
            pack += tokens + filler
            self.pieces.append((dy, dx, offset, size))
            offset += size
        self.sent = offset
        self.rows = TOK + offset
        self.padded = up_to(self.rows, 128)
        self.codes = np.array(codes + [-1] * (self.padded - self.rows), np.int32)
        self.pack = (np.array(pack)[:, None] == np.arange(TOK)[None, :]).astype(np.float32)


def frame_places():
    index = lax.broadcasted_iota(jnp.int32, (TOK, 1), 0)
    place = index >> 1
    row = (place * 43691) >> 19
    return row, place - row * WLON, index & 1


def read_codes(down, right):
    row, col, level = frame_places()
    row_at = row + down
    col_at = col + right
    zone_row = jnp.where(row_at >= WLAT, 1, 0) - jnp.where(row_at < 0, 1, 0)
    zone_col = jnp.where(col_at >= WLON, 1, 0) - jnp.where(col_at < 0, 1, 0)
    place = (row_at - zone_row * WLAT) * WLON + col_at - zone_col * WLON
    return ((zone_row + 1) * 3 + zone_col + 1) * TOK + place * LEV + level


def one_hot(left, right):
    return jnp.where(left == right, 1.0, 0.0).astype(BF16)


def dot(a, b, dims=(((1,), (0,)), ((), ()))):
    return lax.dot_general(a, b, dims, preferred_element_type=F32)


def kernel(
    sizes, halo, mid, out,
    states, final_cot, step_cot, w_qkv, w_out, land_vec, land_sea, ground, shifts,
    pack_halo, pack_mid, pack_out, codes,
    result,
    raw, w_qkv_v, w_out_v, land_vec_v, tables_v, shifts_v, pack_halo_v, pack_mid_v, pack_out_v, codes_v,
    ext_halo, ext_mid, ext_out, send_halo, send_mid, send_out,
    normed_f, proj, att, cot_w, d_proj, d_mixed,
    local_sem, send_sem, recv_sem, go_sem,
):
    n_lat, n_lon = sizes
    features = raw.shape[-1]
    step, lat, lon = lax.axis_index("step"), lax.axis_index("lat"), lax.axis_index("lon")
    late = step == 1

    def around(dy, dx, other=False):
        return (
            1 - step if other else step,
            lax.rem(lat + (dy + n_lat), n_lat),
            lax.rem(lon + (dx + n_lon), n_lon),
        )

    barrier = pltpu.get_barrier_semaphore()
    for dy in (-1, 0, 1):
        for dx in (-1, 0, 1):
            if (dy, dx) != (0, 0):
                pl.semaphore_signal(barrier, inc=1, device_id=around(dy, dx), device_id_type=MESH)
            pl.semaphore_signal(barrier, inc=1, device_id=around(dy, dx, True), device_id_type=MESH)

    local = [
        pltpu.make_async_copy(src, dst, local_sem.at[i])
        for i, (src, dst) in enumerate((
            (states, raw.at[0]),
            (pack_halo, pack_halo_v),
            (final_cot, raw.at[1]),
            (step_cot, raw.at[2]),
            (shifts, shifts_v),
            (codes, codes_v),
            (land_sea, tables_v.at[0]),
            (ground, tables_v.at[1]),
            (land_vec, land_vec_v),
            (w_qkv, w_qkv_v),
            (w_out, w_out_v),
            (pack_out, pack_out_v),
            (pack_mid, pack_mid_v),
        ))
    ]
    (c_state, c_pack, c_final, c_step, c_shift, c_codes, c_land, c_ground, c_vec, c_qkv, c_out, c_pack_out, c_pack_mid) = local
    for copy in local:
        copy.start()

    def sends(which, exchange, buffer, target, other=False):
        made = []
        base = (0, 8, 16, 24, 32)[which]
        for k, (dy, dx, offset, size) in enumerate(exchange.pieces):
            made.append(pltpu.make_async_remote_copy(
                src_ref=buffer.at[pl.ds(offset, size)],
                dst_ref=target.at[pl.ds(TOK + offset, size)],
                send_sem=send_sem.at[base + k],
                recv_sem=recv_sem.at[base + k],
                device_id=around(dy, dx, other),
                device_id_type=MESH,
            ))
        return made

    halo_sends = [sends(i, halo, send_halo.at[i], ext_halo.at[i]) for i in range(3)]
    mid_sends = sends(3, mid, send_mid, ext_mid, True)
    mid_sends.append(pltpu.make_async_remote_copy(
        src_ref=ext_out.at[pl.ds(0, TOK)],
        dst_ref=ext_mid.at[pl.ds(0, TOK)],
        send_sem=send_sem.at[40],
        recv_sem=recv_sem.at[40],
        device_id=around(0, 0, True),
        device_id_type=MESH,
    ))
    out_sends = sends(4, out, send_out, ext_out)

    def pack_field(i):
        field = raw[i].reshape(TOK, features)
        ext_halo[i, pl.ds(0, TOK)] = field
        send_halo[i] = dot(pack_halo_v[...].astype(BF16), field).astype(BF16)

    for i in range(3):
        ext_halo[i, pl.ds(halo.rows, halo.padded - halo.rows)] = jnp.zeros((halo.padded - halo.rows, raw.shape[-1]), BF16)
    ext_mid[pl.ds(mid.rows, mid.padded - mid.rows)] = jnp.zeros((mid.padded - mid.rows, raw.shape[-1]), BF16)
    ext_out[pl.ds(out.rows, out.padded - out.rows)] = jnp.zeros((out.padded - out.rows, raw.shape[-1]), BF16)

    c_state.wait()
    c_pack.wait()
    pack_field(0)
    pl.semaphore_wait(barrier, 17)

    c_final.wait()
    c_step.wait()

    @pl.when(late)
    def _():
        for copy in halo_sends[0]:
            copy.start()
        pack_field(1)
        for copy in halo_sends[1]:
            copy.start()
        pack_field(2)

    c_shift.wait()

    def start_of(row):
        a, b = shifts_v[row, 0], shifts_v[row, 1]
        return jnp.where(a >= 3, a - WLAT, a), jnp.where(b >= 6, b - WLON, b)

    s_late, t_late = start_of(1)
    s_early, t_early = start_of(0)
    s = jnp.where(late, s_late, s_early)
    t = jnp.where(late, t_late, t_early)
    c_codes.wait()
    pick_halo = one_hot(read_codes(s, t), codes_v[0:1, : halo.padded])

    row, col, level = frame_places()
    lat_total, lon_total = tables_v.shape[1], tables_v.shape[2]
    at_row = lat * WLAT + s + row
    at_row = jnp.where(at_row < 0, at_row + lat_total, jnp.where(at_row >= lat_total, at_row - lat_total, at_row))
    at_col = lon * WLON + t + col
    at_col = jnp.where(at_col < 0, at_col + lon_total, jnp.where(at_col >= lon_total, at_col - lon_total, at_col))
    c_land.wait()
    c_ground.wait()
    row_pick = one_hot(at_row, lax.broadcasted_iota(jnp.int32, (TOK, lat_total), 1))
    col_pick = at_col == lax.broadcasted_iota(jnp.int32, (TOK, lon_total), 1)

    def looked_up(i):
        lines = dot(row_pick, tables_v[i].astype(F32).astype(BF16))
        return jnp.sum(jnp.where(col_pick, lines, 0.0), axis=1, keepdims=True)

    land = looked_up(0)
    key_valid = jnp.where(level.astype(F32) >= looked_up(1), 1.0, 0.0)
    shift_lat = jnp.where(s < 0, s + WLAT, s)
    window = jnp.where(s < 0, lax.rem(lat + (n_lat - 1), n_lat), lat)
    first_seam = jnp.where(window == n_lat - 1, WLAT - shift_lat, WLAT)
    lane = lax.broadcasted_iota(jnp.int32, (1, 2 * TOK), 1)
    lane = jnp.where(lane >= TOK, lane - TOK, lane)
    lane_row = ((lane >> 1) * 43691) >> 19
    seam_key = jnp.where(row >= first_seam, 1, 0)
    seam_query = jnp.where(lane_row >= first_seam, 1, 0)
    allowed = jnp.where(seam_key == seam_query, key_valid, 0.0)
    c_vec.wait()

    @pl.when(late)
    def _():
        for copy in halo_sends[0]:
            copy.wait_recv()
        pl.semaphore_signal(go_sem, inc=1, device_id=around(0, 0, True), device_id_type=MESH)

    @pl.when(jnp.logical_not(late))
    def _():
        pl.semaphore_wait(go_sem, 1)
        for copy in halo_sends[0]:
            copy.start()
        for copy in halo_sends[0]:
            copy.wait_recv()

    lifted = dot(pick_halo, ext_halo[0]) + land * land_vec_v[...]
    centred = lifted - jnp.mean(lifted, axis=1, keepdims=True)
    scale = lax.rsqrt(jnp.mean(centred * centred, axis=1, keepdims=True) + 1e-05)
    normed = centred * scale
    normed_f[...] = normed
    c_qkv.wait()
    proj[...] = dot(normed.astype(BF16), w_qkv_v[...]).astype(BF16)
    half = lax.broadcasted_iota(jnp.int32, (TOK, 128), 1) < 64
    zero = jnp.zeros((TOK, 128), BF16)

    def both_heads(pair):
        return jnp.concatenate([jnp.where(half, pair, zero), jnp.where(half, zero, pair)], axis=0)

    def queries(p):
        return both_heads(proj[:, p * 128 : (p + 1) * 128] * 0.125)

    def keys(p):
        return proj[:, features + p * 128 : features + (p + 1) * 128]

    def values(p):
        return proj[:, 2 * features + p * 128 : 2 * features + (p + 1) * 128]

    for p in range(HEADS // 2):
        weights = jnp.exp(dot(keys(p), queries(p), NT)) * allowed
        att[p] = weights * (1.0 / jnp.sum(weights, axis=0, keepdims=True))

    @pl.when(late)
    def _():
        for copy in halo_sends[1]:
            copy.wait_recv()
        for copy in halo_sends[2]:
            copy.start()
        cot_w[...] = dot(pick_halo, ext_halo[1]).astype(BF16)

    @pl.when(jnp.logical_not(late))
    def _():
        pick = one_hot(read_codes(s_early - s_late, t_early - t_late), codes_v[1:2, : mid.padded])
        for copy in mid_sends:
            copy.wait_recv()
        cot_w[...] = dot(pick, ext_mid[...]).astype(BF16)

    c_out.wait()
    d_mixed[...] = dot(cot_w[...], w_out_v[...], NT).astype(BF16)
    for p in range(HEADS // 2):
        d_both = both_heads(d_mixed[:, p * 128 : (p + 1) * 128])
        query, key, attention = queries(p), keys(p), att[p]
        inner = attention * dot(values(p), d_both, NT)
        d_scores = (inner - attention * jnp.sum(inner, axis=0, keepdims=True)).astype(BF16)
        d_query = dot(d_scores, key, TN)
        d_query = jnp.where(half, d_query[:TOK], d_query[TOK:]) * 0.125
        d_proj[:, p * 128 : (p + 1) * 128] = d_query.astype(BF16)
        d_proj[:, features + p * 128 : features + (p + 1) * 128] = dot(d_scores, query).astype(BF16)
        d_proj[:, 2 * features + p * 128 : 2 * features + (p + 1) * 128] = dot(attention.astype(BF16), d_both).astype(BF16)
    d_normed = dot(d_proj[...], w_qkv_v[...], NT).astype(BF16).astype(F32)
    normed = normed_f[...]
    along = jnp.mean(d_normed * normed, axis=1, keepdims=True)
    total = cot_w[...].astype(F32) + scale * (d_normed - jnp.mean(d_normed, axis=1, keepdims=True) - normed * along)
    normed_f[...] = total
    c_pack_out.wait()
    c_pack_mid.wait()

    @pl.when(late)
    def _():
        for copy in halo_sends[2]:
            copy.wait_recv()
        ext_out[pl.ds(0, TOK)] = (normed_f[...] + dot(pick_halo, ext_halo[2])).astype(BF16)
        mid_sends[-1].start()
        send_mid[...] = dot(pack_mid_v[...].astype(BF16), ext_out[pl.ds(0, TOK)]).astype(BF16)
        for copy in mid_sends[:-1]:
            copy.start()

    @pl.when(jnp.logical_not(late))
    def _():
        ext_out[pl.ds(0, TOK)] = normed_f[...].astype(BF16)

    send_out[...] = dot(pack_out_v[...].astype(BF16), ext_out[pl.ds(0, TOK)]).astype(BF16)
    for copy in out_sends:
        copy.start()
    pick_out = one_hot(read_codes(-s, -t), codes_v[2:3, : out.padded])
    for copy in out_sends:
        copy.wait_recv()
    result[...] = dot(pick_out, ext_out[...]).astype(BF16).reshape(result.shape)

    for copy in halo_sends[0] + out_sends:
        copy.wait_send()

    @pl.when(late)
    def _():
        for copy in halo_sends[1] + halo_sends[2] + mid_sends:
            copy.wait_send()


def per_device(sizes, states, final_cot, step_cot, w_qkv, w_out, land_vec, land_sea, ground, shifts):
    halo = Exchange(2, 3, 5, 6)
    mid = Exchange(3, 3, 6, 6)
    out = Exchange(3, 2, 6, 5)
    features = w_qkv.shape[0]
    codes = np.full((8, max(e.padded for e in (halo, mid, out))), -1, np.int32)
    for i, e in enumerate((halo, mid, out)):
        codes[i, : e.padded] = e.codes
    packs = [jnp.asarray(e.pack) for e in (halo, mid, out)]
    any_spec = pl.BlockSpec(memory_space=pl.ANY)

    def field(*shape):
        return pltpu.VMEM(shape, BF16)

    def home(block):
        return jnp.moveaxis(block, 0, 2).reshape(TOK // LEV, LEV, features)

    gradient = pl.pallas_call(
        functools.partial(kernel, sizes, halo, mid, out),
        out_shape=jax.ShapeDtypeStruct((TOK // LEV, LEV, features), BF16),
        in_specs=[any_spec] * 13,
        out_specs=pl.BlockSpec(memory_space=pltpu.VMEM),
        scratch_shapes=[
            field(3, TOK // LEV, LEV, features),
            field(*w_qkv.shape),
            field(*w_out.shape),
            pltpu.VMEM((1, features), F32),
            pltpu.VMEM((2,) + land_sea.shape, jnp.int32),
            pltpu.SMEM(shifts.shape, jnp.int32),
            pltpu.VMEM(halo.pack.shape, F32),
            pltpu.VMEM(mid.pack.shape, F32),
            pltpu.VMEM(out.pack.shape, F32),
            pltpu.VMEM(codes.shape, jnp.int32),
            field(3, halo.padded, features),
            field(mid.padded, features),
            field(out.padded, features),
            field(3, halo.sent, features),
            field(mid.sent, features),
            field(out.sent, features),
            pltpu.VMEM((TOK, features), F32),
            field(TOK, 3 * features),
            pltpu.VMEM((HEADS // 2, TOK, 2 * TOK), F32),
            field(TOK, features),
            field(TOK, 3 * features),
            field(TOK, features),
            pltpu.SemaphoreType.DMA((13,)),
            pltpu.SemaphoreType.DMA((41,)),
            pltpu.SemaphoreType.DMA((41,)),
            pltpu.SemaphoreType.REGULAR,
        ],
        compiler_params=pltpu.CompilerParams(
            collective_id=0, has_side_effects=True, vmem_limit_bytes=60 * 1024 * 1024
        ),
    )(
        home(states[0]), home(final_cot), home(step_cot), w_qkv, w_out, land_vec.reshape(1, features), land_sea, ground, shifts,
        packs[0], packs[1], packs[2], jnp.asarray(codes),
    )
    return jnp.moveaxis(gradient.reshape(WLAT, WLON, LEV, features), 2, 0)[None]


def solution(mesh):
    return jax.shard_map(
        functools.partial(per_device, (mesh.shape["lat"], mesh.shape["lon"])),
        mesh=mesh,
        in_specs=(
            P("step", None, "lat", "lon", None),
            P(None, "lat", "lon", None),
            P(None, "lat", "lon", None),
            P(),
            P(),
            P(),
            P(),
            P(),
            P(),
        ),
        out_specs=P("step", None, "lat", "lon", None),
        check_vma=False,
    )
```

time: 156 us -> 55.4 us (0.36)
  Pallas kernels: 0 us -> 53.6 us
  waiting for transfers between devices: 44.9 us -> 0 us
  starting transfers between devices: 39.9 us -> 0 us
  local copies, waits for them, and re-layouts: 22.8 us -> 1.67 us
  other arithmetic: 16.8 us -> 0 us
  between operations: 16.3 us -> 0.01 us
  matrix products: 13.9 us -> 0 us
    pallas_call x0 -> x1, Pallas kernels: none -> 53.6 us  [per_device(): pl.pallas_call(functools.partial(kernel, sizes, halo, mid, out), out_shap...]
    ppermute x9 -> x0, waiting for transfers between devices: 44.9 us -> none  [the longest x8 42.9 us: shifted(): lax.ppermute(value, axis, [(i, (i + by) % size) for i in range(size)])]
    ppermute x9 -> x0, starting transfers between devices: 39.9 us -> none  [the longest x8 38.6 us: shifted(): lax.ppermute(value, axis, [(i, (i + by) % size) for i in range(size)])]
    dot_general x16 -> x0, matrix products: 13.9 us -> none  [the longest x4 4.53 us: window_branch(): jnp.einsum('wnd,de->wne', windows, w_select, preferred_element_type=jnp.f...]
    another operation x4 -> x0, local copies, waits for them, and re-layouts: 7.07 us -> none
    reshape x4 -> x0, local copies, waits for them, and re-layouts: 6.24 us -> none  [the longest x2 3.67 us: window_branch(): mixed.reshape(windows.shape[0], windows.shape[1], head_count * head_size)]
    concatenate x10 -> x0, other arithmetic: 4.32 us -> none  [the longest x2 2.72 us: layer_adjoint(): jnp.concatenate([rolled, edge_cols], axis=3)]
    unnamed x60 -> x1, local copies, waits for them, and re-layouts: 4.91 us -> 1.67 us
  transfers between devices with their start and end apart: 9 -> 0, of which waited for: 9 -> 0; matrix products, arithmetic and copies ran while one was open for 2% -> 0% of each run, Pallas kernels for 0% -> 0%
where the time goes in v1:
time: 55.4 us; the launch traced here: 55.3 us
  Pallas kernels  53.6 us (97%)
  local copies, waits for them, and re-layouts  1.67 us (3%)
    pallas_call x1, Pallas kernels, per_device(): pl.pallas_call(functools.partial(kernel, sizes, halo, mid, out), out_shap...  53.6 us
    unnamed x1, local copies, waits for them, and re-layouts  1.67 us

profile of v1, /device:TPU:2, one launch (start us, length us, event | category | flops | bytes accessed | tf_op | source)
XLA Modules:
  0.0 55.3 jit_solution(17960145354147879511)
XLA Ops:
  0.0 53.6 %shard_map.127 = bf16[72,2,512]{2,1,0:T(2,128)(2,1)} custom-call(bf16[72,2,512]{2,1,0:T(2,128)(2,1)} %bitcast.18, bf16[72,2,512]{2,1,0:T(2,128)(2,1)} %bitcast.19, bf16[72,2,512]{2,1,0:T(2,128)(2,1)} %bitcast.20, bf16[512,1536]{1,0:T(8,128)(2,1)} %w_qkv.1, bf16[512,512]{1,0:T(8,128)(2,1)} %w_out.1, f32[1,512]{1,0:T(1,128)} %bitcast.21, s32[48,384]{1,0:T(8,128)} %land_sea.1, ...), custom_call_target="tpu_custom_call" | custom-call | tf_op jit(solution)/shard_map/pallas_call | solution.py:345
  53.6 1.7 %copy.15 = bf16[1,2,6,12,512]{4,1,3,2,0:T(2,128)(2,1)} copy(bf16[1,2,6,12,512]{4,1,3,2,0:T(2,128)(2,1)} %bitcast.17) | data formatting | bytes 294912

commit v2 on v1

v2 whole, which is shorter than its diff:
```python
import functools

import jax
import jax.numpy as jnp
import numpy as np
from jax import lax
from jax.experimental import pallas as pl
from jax.experimental.pallas import tpu as pltpu
from jax.sharding import PartitionSpec as P

HEADS = 8
LEV = 2
WLAT = 6
WLON = 12
ROW = WLON * LEV
TOK = WLAT * ROW
LON_CODE = 1000
MESH = pl.DeviceIdType.MESH
F32 = jnp.float32
BF16 = jnp.bfloat16
NT = (((1,), (1,)), ((), ()))
TN = (((0,), (0,)), ((), ()))


def up_to(value, unit):
    return -(-value // unit) * unit


class Exchange:
    def __init__(self, first_rows, last_rows, first_cols, last_cols):
        self.first_cols, self.last_cols = first_cols, last_cols
        self.tail = (WLAT - last_rows) * ROW // 16 * 16
        self.from_before = TOK - self.tail
        self.from_after = up_to(first_rows * ROW, 16)
        self.rows_held = TOK + self.from_before + self.from_after
        self.cols_last = up_to(WLAT * last_cols * LEV, 16)
        self.cols_first = up_to(WLAT * first_cols * LEV, 16)
        self.cols_sent = self.cols_last + self.cols_first
        self.held = self.rows_held + self.cols_sent
        codes = [TOK + token for token in range(TOK)]
        codes += [token for token in range(self.tail, TOK)]
        codes += [2 * TOK + token for token in range(self.from_after)]
        for size, cols in (
            (self.cols_last, range(-last_cols, 0)),
            (self.cols_first, range(WLON, WLON + first_cols)),
        ):
            came = [LON_CODE + (r * 36 + c + WLON) * LEV + l for r in range(WLAT) for c in cols for l in range(LEV)]
            codes += came + [-1] * (size - len(came))
        self.codes = np.array(codes, np.int32)

    def sent_codes(self, down):
        index = lax.broadcasted_iota(jnp.int32, (self.cols_sent, 1), 0)
        is_last = index < self.cols_last
        index = jnp.where(is_last, index, index - self.cols_last)
        place = index >> 1
        row_last, row_first = quotient(place, self.last_cols), quotient(place, self.first_cols)
        row = jnp.where(is_last, row_last, row_first)
        col = place - jnp.where(is_last, row_last * self.last_cols - (WLON - self.last_cols), row_first * self.first_cols)
        return jnp.where(row < WLAT, ROW * (row + down + WLAT) + LEV * col + (index & 1), -2)


def quotient(value, by):
    factor = (1 << 14) // by + 1
    assert all((i * factor) >> 14 == i // by for i in range(TOK + 1))
    return (value * factor) >> 14


def frame_places():
    index = lax.broadcasted_iota(jnp.int32, (TOK, 1), 0)
    place = index >> 1
    row = quotient(place, WLON)
    return row, place - row * WLON, index & 1


def read_codes(down, right):
    row, col, level = frame_places()
    col = col + right
    with_rows = ROW * (row + down + WLAT) + LEV * col + level
    with_cols = LON_CODE + (row * 36 + col + WLON) * LEV + level
    return jnp.where((col >= 0) & (col < WLON), with_rows, with_cols)


def one_hot(left, right):
    return jnp.where(left == right, 1.0, 0.0).astype(BF16)


def dot(a, b, dims=(((1,), (0,)), ((), ()))):
    return lax.dot_general(a, b, dims, preferred_element_type=F32)


def kernel(
    sizes, halo, mid, out,
    states, final_cot, step_cot, w_qkv, w_out, land_vec, land_sea, ground, shifts, codes,
    result,
    raw, w_qkv_v, w_out_v, land_vec_v, tables_v, shifts_v, codes_v,
    ext_halo, ext_mid, ext_out, send_cols, pick_halo, pick_cols,
    normed_f, proj, att, cot_w, d_proj, d_mixed,
    local_sem, send_sem, recv_sem, go_sem,
):
    n_lat, n_lon = sizes
    features = raw.shape[-1]
    step, lat, lon = lax.axis_index("step"), lax.axis_index("lat"), lax.axis_index("lon")
    late = step == 1
    early = step == 0

    def around(dy, dx, other=False):
        return (
            1 - step if other else step,
            lax.rem(lat + (dy + n_lat), n_lat),
            lax.rem(lon + (dx + n_lon), n_lon),
        )

    barrier = pltpu.get_barrier_semaphore()
    partners = [(1, 0), (-1, 0), (0, 1), (0, -1), (0, 0, True), (1, 0, True), (-1, 0, True)]
    for partner in partners:
        pl.semaphore_signal(barrier, inc=1, device_id=around(*partner), device_id_type=MESH)

    local = [
        pltpu.make_async_copy(src, dst, local_sem.at[i])
        for i, (src, dst) in enumerate((
            (states, raw.at[0]),
            (final_cot, raw.at[1]),
            (step_cot, raw.at[2]),
            (shifts, shifts_v),
            (codes, codes_v),
            (land_sea, tables_v.at[0]),
            (ground, tables_v.at[1]),
            (land_vec, land_vec_v),
            (w_qkv, w_qkv_v),
            (w_out, w_out_v),
        ))
    ]
    (c_state, c_final, c_step, c_shift, c_codes, c_land, c_ground, c_vec, c_qkv, c_out) = local
    for copy in local:
        copy.start()

    def remote(slot, src, dst, to):
        return pltpu.make_async_remote_copy(
            src_ref=src, dst_ref=dst, send_sem=send_sem.at[slot], recv_sem=recv_sem.at[slot],
            device_id=around(*to), device_id_type=MESH,
        )

    def row_sends(which, exchange, held, other=False, target=None):
        target = held if target is None else target
        return [
            remote(
                4 * which, held.at[pl.ds(exchange.tail, exchange.from_before)],
                target.at[pl.ds(TOK, exchange.from_before)], (1, 0, other),
            ),
            remote(
                4 * which + 1, held.at[pl.ds(0, exchange.from_after)],
                target.at[pl.ds(TOK + exchange.from_before, exchange.from_after)], (-1, 0, other),
            ),
        ]

    def col_sends(which, exchange, held):
        packed = send_cols.at[which]
        return [
            remote(
                4 * which + 2, packed.at[pl.ds(0, exchange.cols_last)],
                held.at[pl.ds(exchange.rows_held, exchange.cols_last)], (0, 1),
            ),
            remote(
                4 * which + 3, packed.at[pl.ds(exchange.cols_last, exchange.cols_first)],
                held.at[pl.ds(exchange.rows_held + exchange.cols_last, exchange.cols_first)], (0, -1),
            ),
        ]

    def started(copies):
        for copy in copies:
            copy.start()

    def arrived(copies):
        for copy in copies:
            copy.wait_recv()

    halo_rows = [row_sends(i, halo, ext_halo.at[i]) for i in range(3)]
    halo_cols = [col_sends(i, halo, ext_halo.at[i]) for i in range(3)]
    mid_rows = row_sends(3, mid, ext_out, True, ext_mid)
    mid_rows.append(remote(20, ext_out.at[pl.ds(0, TOK)], ext_mid.at[pl.ds(0, TOK)], (0, 0, True)))
    mid_cols = col_sends(3, mid, ext_mid)
    out_rows = row_sends(4, out, ext_out)
    out_cols = col_sends(4, out, ext_out)

    def forward_cols(which, exchange, held, picked):
        rows = dot(picked, held[pl.ds(0, exchange.rows_held)])
        send_cols[which, pl.ds(0, exchange.cols_sent)] = rows.astype(BF16)

    c_state.wait()
    ext_halo[0, pl.ds(0, TOK)] = raw[0].reshape(TOK, features)
    c_final.wait()
    c_step.wait()

    @pl.when(late)
    def _():
        ext_halo[1, pl.ds(0, TOK)] = raw[1].reshape(TOK, features)
        ext_halo[2, pl.ds(0, TOK)] = raw[2].reshape(TOK, features)

    pl.semaphore_wait(barrier, len(partners))

    @pl.when(late)
    def _():
        started(halo_rows[0] + halo_rows[1] + halo_rows[2])

    c_shift.wait()

    def start_of(row):
        a, b = shifts_v[row, 0], shifts_v[row, 1]
        return jnp.where(a >= 3, a - WLAT, a), jnp.where(b >= 6, b - WLON, b)

    s_late, t_late = start_of(1)
    s_early, t_early = start_of(0)
    s = jnp.where(late, s_late, s_early)
    t = jnp.where(late, t_late, t_early)
    c_codes.wait()
    pick_cols[...] = one_hot(halo.sent_codes(s), codes_v[0:1, : halo.rows_held])
    pick_halo[...] = one_hot(read_codes(s, t), codes_v[0:1, : halo.held])

    row, col, level = frame_places()
    lat_total, lon_total = tables_v.shape[1], tables_v.shape[2]
    at_row = lat * WLAT + s + row
    at_row = jnp.where(at_row < 0, at_row + lat_total, jnp.where(at_row >= lat_total, at_row - lat_total, at_row))
    at_col = lon * WLON + t + col
    at_col = jnp.where(at_col < 0, at_col + lon_total, jnp.where(at_col >= lon_total, at_col - lon_total, at_col))
    c_land.wait()
    c_ground.wait()
    row_pick = one_hot(at_row, lax.broadcasted_iota(jnp.int32, (TOK, lat_total), 1))
    col_pick = at_col == lax.broadcasted_iota(jnp.int32, (TOK, lon_total), 1)

    def looked_up(i):
        lines = dot(row_pick, tables_v[i].astype(F32).astype(BF16))
        return jnp.sum(jnp.where(col_pick, lines, 0.0), axis=1, keepdims=True)

    land = looked_up(0)
    key_valid = jnp.where(level.astype(F32) >= looked_up(1), 1.0, 0.0)
    shift_lat = jnp.where(s < 0, s + WLAT, s)
    window = jnp.where(s < 0, lax.rem(lat + (n_lat - 1), n_lat), lat)
    first_seam = jnp.where(window == n_lat - 1, WLAT - shift_lat, WLAT)
    lane = lax.broadcasted_iota(jnp.int32, (1, 2 * TOK), 1)
    lane = jnp.where(lane >= TOK, lane - TOK, lane)
    seam_key = jnp.where(row >= first_seam, 1, 0)
    seam_query = jnp.where(quotient(lane >> 1, WLON) >= first_seam, 1, 0)
    allowed = jnp.where(seam_key == seam_query, key_valid, 0.0)
    c_vec.wait()

    @pl.when(early)
    def _():
        pl.semaphore_wait(go_sem, 1)
        started(halo_rows[0])

    arrived(halo_rows[0])
    forward_cols(0, halo, ext_halo.at[0], pick_cols[...])
    started(halo_cols[0])

    @pl.when(late)
    def _():
        arrived(halo_rows[1])
        pl.semaphore_signal(go_sem, inc=1, device_id=around(0, 0, True), device_id_type=MESH)
        forward_cols(1, halo, ext_halo.at[1], pick_cols[...])
        started(halo_cols[1])

    arrived(halo_cols[0])

    lifted = dot(pick_halo[...], ext_halo[0]) + land * land_vec_v[...]
    centred = lifted - jnp.mean(lifted, axis=1, keepdims=True)
    scale = lax.rsqrt(jnp.mean(centred * centred, axis=1, keepdims=True) + 1e-05)
    normed = centred * scale
    normed_f[...] = normed
    c_qkv.wait()
    proj[...] = dot(normed.astype(BF16), w_qkv_v[...]).astype(BF16)
    half = lax.broadcasted_iota(jnp.int32, (TOK, 128), 1) < 64
    zero = jnp.zeros((TOK, 128), BF16)

    def both_heads(pair):
        return jnp.concatenate([jnp.where(half, pair, zero), jnp.where(half, zero, pair)], axis=0)

    def queries(p):
        return both_heads(proj[:, p * 128 : (p + 1) * 128] * 0.125)

    def keys(p):
        return proj[:, features + p * 128 : features + (p + 1) * 128]

    def values(p):
        return proj[:, 2 * features + p * 128 : 2 * features + (p + 1) * 128]

    for p in range(HEADS // 2):
        weights = jnp.exp(dot(keys(p), queries(p), NT)) * allowed
        att[p] = weights * (1.0 / jnp.sum(weights, axis=0, keepdims=True))

    @pl.when(late)
    def _():
        arrived(halo_rows[2])
        forward_cols(2, halo, ext_halo.at[2], pick_cols[...])
        started(halo_cols[2])
        arrived(halo_cols[1])
        cot_w[...] = dot(pick_halo[...], ext_halo[1]).astype(BF16)

    @pl.when(early)
    def _():
        down, right = s_early - s_late, t_early - t_late
        picked = one_hot(mid.sent_codes(down), codes_v[1:2, : mid.rows_held])
        pick = one_hot(read_codes(down, right), codes_v[1:2, : mid.held])
        arrived(mid_rows)
        forward_cols(3, mid, ext_mid, picked)
        started(mid_cols)
        arrived(mid_cols)
        cot_w[...] = dot(pick, ext_mid[...]).astype(BF16)

    c_out.wait()
    d_mixed[...] = dot(cot_w[...], w_out_v[...], NT).astype(BF16)
    for p in range(HEADS // 2):
        d_both = both_heads(d_mixed[:, p * 128 : (p + 1) * 128])
        query, key, attention = queries(p), keys(p), att[p]
        inner = attention * dot(values(p), d_both, NT)
        d_scores = (inner - attention * jnp.sum(inner, axis=0, keepdims=True)).astype(BF16)
        d_query = dot(d_scores, key, TN)
        d_query = jnp.where(half, d_query[:TOK], d_query[TOK:]) * 0.125
        d_proj[:, p * 128 : (p + 1) * 128] = d_query.astype(BF16)
        d_proj[:, features + p * 128 : features + (p + 1) * 128] = dot(d_scores, query).astype(BF16)
        d_proj[:, 2 * features + p * 128 : 2 * features + (p + 1) * 128] = dot(attention.astype(BF16), d_both).astype(BF16)
    d_normed = dot(d_proj[...], w_qkv_v[...], NT).astype(BF16).astype(F32)
    normed = normed_f[...]
    along = jnp.mean(d_normed * normed, axis=1, keepdims=True)
    total = cot_w[...].astype(F32) + scale * (d_normed - jnp.mean(d_normed, axis=1, keepdims=True) - normed * along)
    normed_f[...] = total

    @pl.when(late)
    def _():
        arrived(halo_cols[2])
        ext_out[pl.ds(0, TOK)] = (normed_f[...] + dot(pick_halo[...], ext_halo[2])).astype(BF16)
        started(mid_rows)

    @pl.when(early)
    def _():
        ext_out[pl.ds(0, TOK)] = normed_f[...].astype(BF16)

    started(out_rows)
    picked = one_hot(out.sent_codes(-s), codes_v[2:3, : out.rows_held])
    pick_out = one_hot(read_codes(-s, -t), codes_v[2:3, : out.held])
    arrived(out_rows)
    forward_cols(4, out, ext_out, picked)
    started(out_cols)
    arrived(out_cols)
    result[...] = dot(pick_out, ext_out[...]).astype(BF16).reshape(result.shape)

    for copy in halo_rows[0] + halo_cols[0] + out_rows + out_cols:
        copy.wait_send()

    @pl.when(late)
    def _():
        for copy in halo_rows[1] + halo_cols[1] + halo_rows[2] + halo_cols[2] + mid_rows:
            copy.wait_send()

    @pl.when(early)
    def _():
        for copy in mid_cols:
            copy.wait_send()


def per_device(sizes, states, final_cot, step_cot, w_qkv, w_out, land_vec, land_sea, ground, shifts):
    halo = Exchange(2, 3, 5, 6)
    mid = Exchange(3, 3, 6, 6)
    out = Exchange(3, 2, 6, 5)
    features = w_qkv.shape[0]
    codes = np.full((8, 512), -1, np.int32)
    for i, e in enumerate((halo, mid, out)):
        codes[i, : e.held] = e.codes
    any_spec = pl.BlockSpec(memory_space=pl.ANY)

    def field(*shape):
        return pltpu.VMEM(shape, BF16)

    def home(block):
        return jnp.moveaxis(block, 0, 2).reshape(TOK // LEV, LEV, features)

    gradient = pl.pallas_call(
        functools.partial(kernel, sizes, halo, mid, out),
        out_shape=jax.ShapeDtypeStruct((TOK // LEV, LEV, features), BF16),
        in_specs=[any_spec] * 10,
        out_specs=pl.BlockSpec(memory_space=pltpu.VMEM),
        scratch_shapes=[
            field(3, TOK // LEV, LEV, features),
            field(*w_qkv.shape),
            field(*w_out.shape),
            pltpu.VMEM((1, features), F32),
            pltpu.VMEM((2,) + land_sea.shape, jnp.int32),
            pltpu.SMEM(shifts.shape, jnp.int32),
            pltpu.VMEM(codes.shape, jnp.int32),
            field(3, halo.held, features),
            field(mid.held, features),
            field(out.held, features),
            field(5, max(e.cols_sent for e in (halo, mid, out)), features),
            field(TOK, halo.held),
            field(halo.cols_sent, halo.rows_held),
            pltpu.VMEM((TOK, features), F32),
            field(TOK, 3 * features),
            pltpu.VMEM((HEADS // 2, TOK, 2 * TOK), F32),
            field(TOK, features),
            field(TOK, 3 * features),
            field(TOK, features),
            pltpu.SemaphoreType.DMA((10,)),
            pltpu.SemaphoreType.DMA((21,)),
            pltpu.SemaphoreType.DMA((21,)),
            pltpu.SemaphoreType.REGULAR,
        ],
        compiler_params=pltpu.CompilerParams(
            collective_id=0, has_side_effects=True, vmem_limit_bytes=60 * 1024 * 1024
        ),
    )(
        home(states[0]), home(final_cot), home(step_cot), w_qkv, w_out, land_vec.reshape(1, features),
        land_sea, ground, shifts, jnp.asarray(codes),
    )
    return jnp.moveaxis(gradient.reshape(WLAT, WLON, LEV, features), 2, 0)[None]


def solution(mesh):
    return jax.shard_map(
        functools.partial(per_device, (mesh.shape["lat"], mesh.shape["lon"])),
        mesh=mesh,
        in_specs=(
            P("step", None, "lat", "lon", None),
            P(None, "lat", "lon", None),
            P(None, "lat", "lon", None),
            P(),
            P(),
            P(),
            P(),
            P(),
            P(),
        ),
        out_specs=P("step", None, "lat", "lon", None),
        check_vma=False,
    )
```

time: 55.4 us -> 51.9 us (0.937)
  the two profiles are of different devices: /device:TPU:2 before, /device:TPU:28 now
where the time goes in v2:
time: 51.9 us; the launch traced here: 51.7 us
  Pallas kernels  50 us (96%)
  local copies, waits for them, and re-layouts  1.67 us (3%)
    pallas_call x1, Pallas kernels, per_device(): pl.pallas_call(functools.partial(kernel, sizes, halo, mid, out), out_shap...  50 us
    unnamed x1, local copies, waits for them, and re-layouts  1.67 us

profile of v2, /device:TPU:28, one launch (start us, length us, event | category | flops | bytes accessed | tf_op | source)
XLA Modules:
  0.0 51.7 jit_solution(12739524317526261595)
XLA Ops:
  0.0 50.0 %shard_map.100 = bf16[72,2,512]{2,1,0:T(2,128)(2,1)} custom-call(bf16[72,2,512]{2,1,0:T(2,128)(2,1)} %bitcast.18, bf16[72,2,512]{2,1,0:T(2,128)(2,1)} %bitcast.19, bf16[72,2,512]{2,1,0:T(2,128)(2,1)} %bitcast.20, bf16[512,1536]{1,0:T(8,128)(2,1)} %w_qkv.1, bf16[512,512]{1,0:T(8,128)(2,1)} %w_out.1, f32[1,512]{1,0:T(1,128)} %bitcast.21, s32[48,384]{1,0:T(8,128)} %land_sea.1, ...), custom_call_target="tpu_custom_call" | custom-call | tf_op jit(solution)/shard_map/pallas_call | solution.py:376
  50.0 1.7 %copy.12 = bf16[1,2,6,12,512]{4,1,3,2,0:T(2,128)(2,1)} copy(bf16[1,2,6,12,512]{4,1,3,2,0:T(2,128)(2,1)} %bitcast.17) | data formatting | bytes 294912

commit v3 on v2

--- a/solution.py
+++ b/solution.py
@@ -94,7 +94,7 @@
     result,
     raw, w_qkv_v, w_out_v, land_vec_v, tables_v, shifts_v, codes_v,
     ext_halo, ext_mid, ext_out, send_cols, pick_halo, pick_cols,
-    normed_f, proj, att, cot_w, d_proj, d_mixed,
+    normed_f, proj, att, cot_f, d_proj, d_mixed, direct,
     local_sem, send_sem, recv_sem, go_sem,
 ):
     n_lat, n_lon = sizes
@@ -119,7 +119,6 @@
         pltpu.make_async_copy(src, dst, local_sem.at[i])
         for i, (src, dst) in enumerate((
             (states, raw.at[0]),
-            (final_cot, raw.at[1]),
             (step_cot, raw.at[2]),
             (shifts, shifts_v),
             (codes, codes_v),
@@ -130,9 +129,14 @@
             (w_out, w_out_v),
         ))
     ]
-    (c_state, c_final, c_step, c_shift, c_codes, c_land, c_ground, c_vec, c_qkv, c_out) = local
+    (c_state, c_step, c_shift, c_codes, c_land, c_ground, c_vec, c_qkv, c_out) = local
+    c_final = pltpu.make_async_copy(final_cot, raw.at[1], local_sem.at[len(local)])
     for copy in local:
         copy.start()
+
+    @pl.when(late)
+    def _():
+        c_final.start()
 
     def remote(slot, src, dst, to):
         return pltpu.make_async_remote_copy(
@@ -174,13 +178,13 @@
         for copy in copies:
             copy.wait_recv()
 
-    halo_rows = [row_sends(i, halo, ext_halo.at[i]) for i in range(3)]
-    halo_cols = [col_sends(i, halo, ext_halo.at[i]) for i in range(3)]
-    mid_rows = row_sends(3, mid, ext_out, True, ext_mid)
-    mid_rows.append(remote(20, ext_out.at[pl.ds(0, TOK)], ext_mid.at[pl.ds(0, TOK)], (0, 0, True)))
-    mid_cols = col_sends(3, mid, ext_mid)
-    out_rows = row_sends(4, out, ext_out)
-    out_cols = col_sends(4, out, ext_out)
+    halo_rows = [row_sends(i, halo, ext_halo.at[i]) for i in range(2)]
+    halo_cols = [col_sends(i, halo, ext_halo.at[i]) for i in range(2)]
+    mid_rows = row_sends(2, mid, ext_out, True, ext_mid)
+    mid_rows.append(remote(16, ext_out.at[pl.ds(0, TOK)], ext_mid.at[pl.ds(0, TOK)], (0, 0, True)))
+    mid_cols = col_sends(2, mid, ext_mid)
+    out_rows = row_sends(3, out, ext_out)
+    out_cols = col_sends(3, out, ext_out)
 
     def forward_cols(which, exchange, held, picked):
         rows = dot(picked, held[pl.ds(0, exchange.rows_held)])
@@ -188,19 +192,24 @@
 
     c_state.wait()
     ext_halo[0, pl.ds(0, TOK)] = raw[0].reshape(TOK, features)
-    c_final.wait()
+    pl.semaphore_wait(barrier, len(partners))
+
+    @pl.when(late)
+    def _():
+        started(halo_rows[0])
+
     c_step.wait()
 
     @pl.when(late)
     def _():
+        c_final.wait()
         ext_halo[1, pl.ds(0, TOK)] = raw[1].reshape(TOK, features)
-        ext_halo[2, pl.ds(0, TOK)] = raw[2].reshape(TOK, features)
-
-    pl.semaphore_wait(barrier, len(partners))
-
-    @pl.when(late)
-    def _():
-        started(halo_rows[0] + halo_rows[1] + halo_rows[2])
+        direct[...] = raw[2].reshape(TOK, features)
+
+    @pl.when(early)
+    def _():
+        ext_halo[1, pl.ds(0, TOK)] = raw[2].reshape(TOK, features)
+        direct[...] = jnp.zeros((TOK, features), BF16)
 
     c_shift.wait()
 
@@ -246,19 +255,16 @@
     @pl.when(early)
     def _():
         pl.semaphore_wait(go_sem, 1)
-        started(halo_rows[0])
+        started(halo_rows[0] + halo_rows[1])
 
     arrived(halo_rows[0])
+
+    @pl.when(late)
+    def _():
+        started(halo_rows[1])
+
     forward_cols(0, halo, ext_halo.at[0], pick_cols[...])
     started(halo_cols[0])
-
-    @pl.when(late)
-    def _():
-        arrived(halo_rows[1])
-        pl.semaphore_signal(go_sem, inc=1, device_id=around(0, 0, True), device_id_type=MESH)
-        forward_cols(1, halo, ext_halo.at[1], pick_cols[...])
-        started(halo_cols[1])
-
     arrived(halo_cols[0])
 
     lifted = dot(pick_halo[...], ext_halo[0]) + land * land_vec_v[...]
@@ -268,6 +274,16 @@
     normed_f[...] = normed
     c_qkv.wait()
     proj[...] = dot(normed.astype(BF16), w_qkv_v[...]).astype(BF16)
+
+    arrived(halo_rows[1])
+
+    @pl.when(late)
+    def _():
+        pl.semaphore_signal(go_sem, inc=1, device_id=around(0, 0, True), device_id_type=MESH)
+
+    forward_cols(1, halo, ext_halo.at[1], pick_cols[...])
+    started(halo_cols[1])
+
     half = lax.broadcasted_iota(jnp.int32, (TOK, 128), 1) < 64
     zero = jnp.zeros((TOK, 128), BF16)
 
@@ -287,13 +303,8 @@
         weights = jnp.exp(dot(keys(p), queries(p), NT)) * allowed
         att[p] = weights * (1.0 / jnp.sum(weights, axis=0, keepdims=True))
 
-    @pl.when(late)
-    def _():
-        arrived(halo_rows[2])
-        forward_cols(2, halo, ext_halo.at[2], pick_cols[...])
-        started(halo_cols[2])
-        arrived(halo_cols[1])
-        cot_w[...] = dot(pick_halo[...], ext_halo[1]).astype(BF16)
+    arrived(halo_cols[1])
+    cot_f[...] = dot(pick_halo[...], ext_halo[1])
 
     @pl.when(early)
     def _():
@@ -301,13 +312,16 @@
         picked = one_hot(mid.sent_codes(down), codes_v[1:2, : mid.rows_held])
         pick = one_hot(read_codes(down, right), codes_v[1:2, : mid.held])
         arrived(mid_rows)
-        forward_cols(3, mid, ext_mid, picked)
+        pl.semaphore_signal(go_sem, inc=1, device_id=around(0, 0, True), device_id_type=MESH)
+        forward_cols(2, mid, ext_mid, picked)
         started(mid_cols)
         arrived(mid_cols)
-        cot_w[...] = dot(pick, ext_mid[...]).astype(BF16)
+        cot_f[...] += dot(pick, ext_mid[...])
+
+    cot_w = cot_f[...].astype(BF16)
 
     c_out.wait()
-    d_mixed[...] = dot(cot_w[...], w_out_v[...], NT).astype(BF16)
+    d_mixed[...] = dot(cot_w, w_out_v[...], NT).astype(BF16)
     for p in range(HEADS // 2):
         d_both = both_heads(d_mixed[:, p * 128 : (p + 1) * 128])
         query, key, attention = queries(p), keys(p), att[p]
@@ -321,34 +335,30 @@
     d_normed = dot(d_proj[...], w_qkv_v[...], NT).astype(BF16).astype(F32)
     normed = normed_f[...]
     along = jnp.mean(d_normed * normed, axis=1, keepdims=True)
-    total = cot_w[...].astype(F32) + scale * (d_normed - jnp.mean(d_normed, axis=1, keepdims=True) - normed * along)
-    normed_f[...] = total
-
-    @pl.when(late)
-    def _():
-        arrived(halo_cols[2])
-        ext_out[pl.ds(0, TOK)] = (normed_f[...] + dot(pick_halo[...], ext_halo[2])).astype(BF16)
+    total = cot_w.astype(F32) + scale * (d_normed - jnp.mean(d_normed, axis=1, keepdims=True) - normed * along)
+    ext_out[pl.ds(0, TOK)] = total.astype(BF16)
+
+    @pl.when(late)
+    def _():
         started(mid_rows)
-
-    @pl.when(early)
-    def _():
-        ext_out[pl.ds(0, TOK)] = normed_f[...].astype(BF16)
+        pl.semaphore_wait(go_sem, 1)
 
     started(out_rows)
     picked = one_hot(out.sent_codes(-s), codes_v[2:3, : out.rows_held])
     pick_out = one_hot(read_codes(-s, -t), codes_v[2:3, : out.held])
     arrived(out_rows)
-    forward_cols(4, out, ext_out, picked)
+    forward_cols(3, out, ext_out, picked)
     started(out_cols)
     arrived(out_cols)
-    result[...] = dot(pick_out, ext_out[...]).astype(BF16).reshape(result.shape)
-
-    for copy in halo_rows[0] + halo_cols[0] + out_rows + out_cols:
+    home = dot(pick_out, ext_out[...]) + direct[...].astype(F32)
+    result[...] = home.astype(BF16).reshape(result.shape)
+
+    for copy in halo_rows[0] + halo_cols[0] + halo_rows[1] + halo_cols[1] + out_rows + out_cols:
         copy.wait_send()
 
     @pl.when(late)
     def _():
-        for copy in halo_rows[1] + halo_cols[1] + halo_rows[2] + halo_cols[2] + mid_rows:
+        for copy in mid_rows:
             copy.wait_send()
 
     @pl.when(early)
@@ -365,7 +375,7 @@
     codes = np.full((8, 512), -1, np.int32)
     for i, e in enumerate((halo, mid, out)):
         codes[i, : e.held] = e.codes
-    any_spec = pl.BlockSpec(memory_space=pl.ANY)
+    held_spec = pl.BlockSpec(memory_space=pltpu.HBM)
 
     def field(*shape):
         return pltpu.VMEM(shape, BF16)
@@ -376,7 +386,7 @@
     gradient = pl.pallas_call(
         functools.partial(kernel, sizes, halo, mid, out),
         out_shape=jax.ShapeDtypeStruct((TOK // LEV, LEV, features), BF16),
-        in_specs=[any_spec] * 10,
+        in_specs=[held_spec] * 10,
         out_specs=pl.BlockSpec(memory_space=pltpu.VMEM),
         scratch_shapes=[
             field(3, TOK // LEV, LEV, features),
@@ -386,21 +396,22 @@
             pltpu.VMEM((2,) + land_sea.shape, jnp.int32),
             pltpu.SMEM(shifts.shape, jnp.int32),
             pltpu.VMEM(codes.shape, jnp.int32),
-            field(3, halo.held, features),
+            field(2, halo.held, features),
             field(mid.held, features),
             field(out.held, features),
-            field(5, max(e.cols_sent for e in (halo, mid, out)), features),
+            field(4, max(e.cols_sent for e in (halo, mid, out)), features),
             field(TOK, halo.held),
             field(halo.cols_sent, halo.rows_held),
             pltpu.VMEM((TOK, features), F32),
             field(TOK, 3 * features),
             pltpu.VMEM((HEADS // 2, TOK, 2 * TOK), F32),
-            field(TOK, features),
+            pltpu.VMEM((TOK, features), F32),
             field(TOK, 3 * features),
             field(TOK, features),
+            field(TOK, features),
             pltpu.SemaphoreType.DMA((10,)),
-            pltpu.SemaphoreType.DMA((21,)),
-            pltpu.SemaphoreType.DMA((21,)),
+            pltpu.SemaphoreType.DMA((17,)),
+            pltpu.SemaphoreType.DMA((17,)),
             pltpu.SemaphoreType.REGULAR,
         ],
         compiler_params=pltpu.CompilerParams(

time: 51.9 us -> 59.3 us (1.14)
  the two profiles are of different devices: /device:TPU:28 before, /device:TPU:2 now
where the time goes in v3:
time: 59.3 us; the launch traced here: 59.2 us
  Pallas kernels  57.5 us (97%)
  local copies, waits for them, and re-layouts  1.67 us (3%)
    pallas_call x1, Pallas kernels, per_device(): pl.pallas_call(functools.partial(kernel, sizes, halo, mid, out), out_shap...  57.5 us
    unnamed x1, local copies, waits for them, and re-layouts  1.67 us

profile of v3, /device:TPU:2, one launch (start us, length us, event | category | flops | bytes accessed | tf_op | source)
XLA Modules:
  0.0 59.2 jit_solution(9236837358104518525)
XLA Ops:
  0.0 57.5 %shard_map.100 = bf16[72,2,512]{2,1,0:T(2,128)(2,1)} custom-call(bf16[72,2,512]{2,1,0:T(2,128)(2,1)} %bitcast.18, bf16[72,2,512]{2,1,0:T(2,128)(2,1)} %bitcast.19, bf16[72,2,512]{2,1,0:T(2,128)(2,1)} %bitcast.20, bf16[512,1536]{1,0:T(8,128)(2,1)} %w_qkv.1, bf16[512,512]{1,0:T(8,128)(2,1)} %w_out.1, f32[1,512]{1,0:T(1,128)} %bitcast.21, s32[48,384]{1,0:T(8,128)} %land_sea.1, ...), custom_call_target="tpu_custom_call" | custom-call | tf_op jit(solution)/shard_map/pallas_call | solution.py:386
  57.5 1.7 %copy.12 = bf16[1,2,6,12,512]{4,1,3,2,0:T(2,128)(2,1)} copy(bf16[1,2,6,12,512]{4,1,3,2,0:T(2,128)(2,1)} %bitcast.17) | data formatting | bytes 294912

commit v4 on v3

v4 whole, which is shorter than its diff:
```python
import functools

import jax
import jax.numpy as jnp
import numpy as np
from jax import lax
from jax.experimental import pallas as pl
from jax.experimental.pallas import tpu as pltpu
from jax.sharding import PartitionSpec as P

HEADS = 8
LEV = 2
WLAT = 6
WLON = 12
ROW = WLON * LEV
TOK = WLAT * ROW
MESH = pl.DeviceIdType.MESH
F32 = jnp.float32
BF16 = jnp.bfloat16
NT = (((1,), (1,)), ((), ()))
TN = (((0,), (0,)), ((), ()))


def up_to(value, unit):
    return -(-value // unit) * unit


class Exchange:
    def __init__(self, first_rows, last_rows, first_cols, last_cols):
        rows = {-1: range(first_rows), 0: range(WLAT), 1: range(WLAT - last_rows, WLAT)}
        cols = {-1: range(first_cols), 0: range(WLON), 1: range(WLON - last_cols, WLON)}
        self.pieces = []
        packed, codes = [], list(range(4 * TOK, 5 * TOK))
        offset = 0
        for dy, dx in ((1, 1), (1, -1), (-1, 1), (-1, -1), (1, 0), (-1, 0), (0, 1), (0, -1)):
            tokens = [(r * WLON + c) * LEV + l for r in rows[dy] for c in cols[dx] for l in range(LEV)]
            if not tokens:
                continue
            size = up_to(len(tokens), 16)
            zone = (1 - dy) * 3 + 1 - dx
            filler = [-1] * (size - len(tokens))
            codes += [zone * TOK + token for token in tokens] + filler
            packed += tokens + filler
            self.pieces.append((dy, dx, offset, size))
            offset += size
        self.sent = offset
        self.held = TOK + offset
        self.codes, self.packed = np.array(codes, np.int32), np.array(packed, np.int32)


def quotient(value, by):
    factor = (1 << 14) // by + 1
    assert all((i * factor) >> 14 == i // by for i in range(TOK + 1))
    return (value * factor) >> 14


def frame_places():
    index = lax.broadcasted_iota(jnp.int32, (TOK, 1), 0)
    place = index >> 1
    row = quotient(place, WLON)
    return row, place - row * WLON, index & 1


def read_codes(down, right):
    row, col, level = frame_places()
    row, col = row + down, col + right
    zone_row = jnp.where(row >= WLAT, 1, 0) - jnp.where(row < 0, 1, 0)
    zone_col = jnp.where(col >= WLON, 1, 0) - jnp.where(col < 0, 1, 0)
    place = (row - zone_row * WLAT) * WLON + col - zone_col * WLON
    return ((zone_row + 1) * 3 + zone_col + 1) * TOK + place * LEV + level


def one_hot(left, right):
    return jnp.where(left == right, 1.0, 0.0).astype(BF16)


def dot(a, b, dims=(((1,), (0,)), ((), ()))):
    return lax.dot_general(a, b, dims, preferred_element_type=F32)


def kernel(
    sizes, starts, halo, mid, out,
    states, final_cot, step_cot, w_qkv, w_out, land_vec, land_sea, ground, shifts, codes,
    result,
    raw, w_qkv_v, w_out_v, land_vec_v, tables_v, shifts_v, codes_v,
    ext_halo, ext_mid, ext_out, send_halo, send_mid, send_out,
    normed_f, proj, att, cot_f, d_proj, d_mixed, direct,
    local_sem, send_sem, recv_sem,
):
    n_lat, n_lon = sizes
    features = w_qkv.shape[0]
    pairs = HEADS // 2
    step, lat, lon = lax.axis_index("step"), lax.axis_index("lat"), lax.axis_index("lon")
    late = step == 1
    early = step == 0

    def around(dy, dx, other=False):
        return (
            1 - step if other else step,
            lax.rem(lat + (dy + n_lat), n_lat),
            lax.rem(lon + (dx + n_lon), n_lon),
        )

    to_early = [(0, 0)] + [(dy, dx) for dy, dx, _, _ in mid.pieces]
    to_same = sorted(
        {(dy, dx) for dy, dx, _, _ in halo.pieces + out.pieces} | {(-dy, -dx) for dy, dx, _, _ in halo.pieces + out.pieces}
    )
    sign = 2 * step - 1
    barrier = pltpu.get_barrier_semaphore()
    for dy, dx in to_same:
        pl.semaphore_signal(barrier, inc=1, device_id=around(dy, dx), device_id_type=MESH)
    for dy, dx in to_early:
        pl.semaphore_signal(barrier, inc=1, device_id=around(dy * sign, dx * sign, True), device_id_type=MESH)

    local = [
        pltpu.make_async_copy(src, dst, local_sem.at[i])
        for i, (src, dst) in enumerate((
            (states, raw.at[0]),
            (codes, codes_v),
            (step_cot, raw.at[2]),
            (shifts, shifts_v),
            (land_sea, tables_v.at[0]),
            (ground, tables_v.at[1]),
            (land_vec, land_vec_v),
            (w_qkv, w_qkv_v),
            (w_out, w_out_v),
            (final_cot, raw.at[1]),
        ))
    ]
    (c_state, c_codes, c_step, c_shift, c_land, c_ground, c_vec, c_qkv, c_out, c_final) = local
    for copy in local:
        copy.start()

    def remotes(first, exchange, src, dst, other=False):
        return [
            pltpu.make_async_remote_copy(
                src_ref=src.at[pl.ds(offset, size)], dst_ref=dst.at[pl.ds(TOK + offset, size)],
                send_sem=send_sem.at[first + k], recv_sem=recv_sem.at[first + k],
                device_id=around(dy, dx, other), device_id_type=MESH,
            )
            for k, (dy, dx, offset, size) in enumerate(exchange.pieces)
        ]

    halo_sends = [remotes(8 * i, halo, send_halo.at[i], ext_halo.at[i]) for i in range(2)]
    out_sends = remotes(16, out, send_out, ext_out)
    mid_sends = [pltpu.make_async_remote_copy(
        src_ref=ext_out.at[pl.ds(0, TOK)], dst_ref=ext_mid.at[pl.ds(0, TOK)],
        send_sem=send_sem.at[32], recv_sem=recv_sem.at[32], device_id=around(0, 0, True), device_id_type=MESH,
    )] + remotes(24, mid, send_mid, ext_mid, True)

    def started(copies):
        for copy in copies:
            copy.start()

    def arrived(copies):
        for copy in copies:
            copy.wait_recv()

    def packing(row, exchange):
        token = lax.broadcasted_iota(jnp.int32, (TOK, exchange.sent), 0)
        return one_hot(token, codes_v[row : row + 1, : exchange.sent])

    c_codes.wait()
    pack_halo = packing(3, halo)
    c_state.wait()
    c_step.wait()
    c_final.wait()
    ext_halo[0, pl.ds(0, TOK)] = raw[0].reshape(TOK, features)
    send_halo[0] = dot(pack_halo, ext_halo[0, pl.ds(0, TOK)], TN).astype(BF16)
    pl.semaphore_wait(barrier, len(to_same) + len(to_early))
    started(halo_sends[0])
    ext_halo[1, pl.ds(0, TOK)] = raw[2 - step].reshape(TOK, features)
    send_halo[1] = dot(pack_halo, ext_halo[1, pl.ds(0, TOK)], TN).astype(BF16)
    started(halo_sends[1])

    @pl.when(late)
    def _():
        direct[...] = raw[2].reshape(TOK, features)

    @pl.when(early)
    def _():
        direct[...] = jnp.zeros((TOK, features), BF16)

    c_shift.wait()
    s_early, s_late = starts
    t_early, t_late = (jnp.where(b >= 6, b - WLON, b) for b in (shifts_v[0, 1], shifts_v[1, 1]))
    s = jnp.where(late, s_late, s_early)
    t = jnp.where(late, t_late, t_early)
    pick_halo = one_hot(read_codes(s, t), codes_v[0:1, : halo.held])

    row, col, level = frame_places()
    lat_total, lon_total = tables_v.shape[1], tables_v.shape[2]
    at_row = lat * WLAT + s + row
    at_row = jnp.where(at_row < 0, at_row + lat_total, jnp.where(at_row >= lat_total, at_row - lat_total, at_row))
    at_col = lon * WLON + t + col
    at_col = jnp.where(at_col < 0, at_col + lon_total, jnp.where(at_col >= lon_total, at_col - lon_total, at_col))
    c_land.wait()
    c_ground.wait()
    row_pick = one_hot(at_row, lax.broadcasted_iota(jnp.int32, (TOK, lat_total), 1))
    col_pick = at_col == lax.broadcasted_iota(jnp.int32, (TOK, lon_total), 1)

    def looked_up(table):
        lines = dot(row_pick, table.astype(F32).astype(BF16))
        return jnp.sum(jnp.where(col_pick, lines, 0.0), axis=1, keepdims=True)

    both = looked_up(tables_v[0] + 2 * tables_v[1])
    ground_at = jnp.where(both >= 1.5, 1.0, 0.0)
    land = both - 2.0 * ground_at
    key_valid = jnp.where(level.astype(F32) >= ground_at, 1.0, 0.0)
    shift_lat = jnp.where(s < 0, s + WLAT, s)
    window = jnp.where(s < 0, lax.rem(lat + (n_lat - 1), n_lat), lat)
    first_seam = jnp.where(window == n_lat - 1, WLAT - shift_lat, WLAT)
    lane = lax.broadcasted_iota(jnp.int32, (1, 2 * TOK), 1)
    lane = jnp.where(lane >= TOK, lane - TOK, lane)
    seam_key = jnp.where(row >= first_seam, 1, 0)
    seam_query = jnp.where(quotient(lane >> 1, WLON) >= first_seam, 1, 0)
    allowed = jnp.where(seam_key == seam_query, key_valid, 0.0)
    c_vec.wait()
    c_qkv.wait()
    arrived(halo_sends[0])

    lifted = dot(pick_halo, ext_halo[0]) + land * land_vec_v[...]
    centred = lifted - jnp.mean(lifted, axis=1, keepdims=True)
    scale = lax.rsqrt(jnp.mean(centred * centred, axis=1, keepdims=True) + 1e-05)
    normed = centred * scale
    normed_f[...] = normed
    projected = dot(normed.astype(BF16), w_qkv_v[...]).astype(BF16)
    for p in range(3 * pairs):
        proj[p] = projected[:, p * 128 : (p + 1) * 128]
    half = lax.broadcasted_iota(jnp.int32, (TOK, 128), 1) < 64
    zero = jnp.zeros((TOK, 128), BF16)

    def both_heads(pair):
        return jnp.concatenate([jnp.where(half, pair, zero), jnp.where(half, zero, pair)], axis=0)

    @pl.loop(0, pairs)
    def _(p):
        weights = jnp.exp(dot(proj[pairs + p], both_heads(proj[p] * 0.125), NT)) * allowed
        att[p] = weights * (1.0 / jnp.sum(weights, axis=0, keepdims=True))

    arrived(halo_sends[1])
    cot_f[...] = dot(pick_halo, ext_halo[1])
    c_out.wait()

    @pl.when(early)
    def _():
        pick = one_hot(read_codes(s_early - s_late, t_early - t_late), codes_v[1:2, : mid.held])
        arrived(mid_sends)
        cot_f[...] += dot(pick, ext_mid[...])

    cot_w = cot_f[...].astype(BF16)

    d_all = dot(cot_w, w_out_v[...], NT).astype(BF16)
    for p in range(pairs):
        d_mixed[p] = d_all[:, p * 128 : (p + 1) * 128]

    @pl.loop(0, pairs)
    def _(p):
        d_both = both_heads(d_mixed[p])
        attention = att[p]
        inner = attention * dot(proj[2 * pairs + p], d_both, NT)
        d_scores = (inner - attention * jnp.sum(inner, axis=0, keepdims=True)).astype(BF16)
        d_query = dot(d_scores, proj[pairs + p], TN)
        d_query = jnp.where(half, d_query[:TOK], d_query[TOK:]) * 0.125
        d_proj[p] = d_query.astype(BF16)
        d_proj[pairs + p] = dot(d_scores, both_heads(proj[p] * 0.125)).astype(BF16)
        d_proj[2 * pairs + p] = dot(attention.astype(BF16), d_both).astype(BF16)

    d_all = jnp.concatenate([d_proj[p] for p in range(3 * pairs)], axis=1)
    d_normed = dot(d_all, w_qkv_v[...], NT).astype(BF16).astype(F32)
    normed = normed_f[...]
    along = jnp.mean(d_normed * normed, axis=1, keepdims=True)
    total = cot_w.astype(F32) + scale * (d_normed - jnp.mean(d_normed, axis=1, keepdims=True) - normed * along)
    ext_out[pl.ds(0, TOK)] = total.astype(BF16)

    @pl.when(late)
    def _():
        mid_sends[0].start()
        send_mid[...] = dot(packing(4, mid), ext_out[pl.ds(0, TOK)], TN).astype(BF16)
        started(mid_sends[1:])

    send_out[...] = dot(packing(5, out), ext_out[pl.ds(0, TOK)], TN).astype(BF16)
    started(out_sends)
    pick_out = one_hot(read_codes(-s, -t), codes_v[2:3, : out.held])
    arrived(out_sends)
    home = dot(pick_out, ext_out[...]) + direct[...].astype(F32)
    result[...] = home.astype(BF16).reshape(result.shape)

    for copy in halo_sends[0] + halo_sends[1] + out_sends:
        copy.wait_send()

    @pl.when(late)
    def _():
        for copy in mid_sends:
            copy.wait_send()


def variant(sizes, number, starts, states, final_cot, step_cot, w_qkv, w_out, land_vec, land_sea, ground, shifts):
    before, after = max(-min(starts), 0), max(max(starts), 0)
    apart = starts[0] - starts[1]
    halo = Exchange(after, before, 5, 6)
    mid = Exchange(max(apart, 0), max(-apart, 0), 6, 6)
    out = Exchange(before, after, 6, 5)
    features = w_qkv.shape[0]
    codes = np.full((8, 512), -1, np.int32)
    for i, e in enumerate((halo, mid, out)):
        codes[i, : e.held] = e.codes
        codes[3 + i, : e.sent] = e.packed
    held_spec = pl.BlockSpec(memory_space=pltpu.HBM)

    def field(*shape):
        return pltpu.VMEM(shape, BF16)

    def home(block):
        return jnp.moveaxis(block, 0, 2).reshape(TOK // LEV, LEV, features)

    gradient = pl.pallas_call(
        functools.partial(kernel, sizes, starts, halo, mid, out),
        out_shape=jax.ShapeDtypeStruct((TOK // LEV, LEV, features), BF16),
        in_specs=[held_spec] * 10,
        out_specs=pl.BlockSpec(memory_space=pltpu.VMEM),
        scratch_shapes=[
            field(3, TOK // LEV, LEV, features),
            field(*w_qkv.shape),
            field(*w_out.shape),
            pltpu.VMEM((1, features), F32),
            pltpu.VMEM((2,) + land_sea.shape, jnp.int32),
            pltpu.SMEM(shifts.shape, jnp.int32),
            pltpu.VMEM(codes.shape, jnp.int32),
            field(2, halo.held, features),
            field(mid.held, features),
            field(out.held, features),
            field(2, halo.sent, features),
            field(mid.sent, features),
            field(out.sent, features),
            pltpu.VMEM((TOK, features), F32),
            field(3 * HEADS // 2, TOK, 128),
            pltpu.VMEM((HEADS // 2, TOK, 2 * TOK), F32),
            pltpu.VMEM((TOK, features), F32),
            field(3 * HEADS // 2, TOK, 128),
            field(HEADS // 2, TOK, 128),
            field(TOK, features),
            pltpu.SemaphoreType.DMA((10,)),
            pltpu.SemaphoreType.DMA((33,)),
            pltpu.SemaphoreType.DMA((33,)),
        ],
        compiler_params=pltpu.CompilerParams(
            collective_id=number, has_side_effects=True, vmem_limit_bytes=60 * 1024 * 1024
        ),
    )(
        home(states[0]), home(final_cot), home(step_cot), w_qkv, w_out, land_vec.reshape(1, features),
        land_sea, ground, shifts, jnp.asarray(codes),
    )
    return jnp.moveaxis(gradient.reshape(WLAT, WLON, LEV, features), 2, 0)[None]


def per_device(sizes, *operands):
    others = (1, 2, 3 - WLAT, 4 - WLAT, -1)
    pairs = [(start, -1) for start in others] + [(-1, start) for start in others[:-1]]
    shifts = operands[-1]
    case = jnp.where(shifts[1, 0] == 5, shifts[0, 0] - 1, shifts[1, 0] + 4)
    cases = [functools.partial(variant, sizes, number, pair) for number, pair in enumerate(pairs)]
    return lax.switch(case, cases, *operands)


def solution(mesh):
    return jax.shard_map(
        functools.partial(per_device, (mesh.shape["lat"], mesh.shape["lon"])),
        mesh=mesh,
        in_specs=(
            P("step", None, "lat", "lon", None),
            P(None, "lat", "lon", None),
            P(None, "lat", "lon", None),
            P(),
            P(),
            P(),
            P(),
            P(),
            P(),
        ),
        out_specs=P("step", None, "lat", "lon", None),
        check_vma=False,
    )
```

time: 59.3 us -> 49.6 us (0.84)
  Pallas kernels: 57.5 us -> 45 us
  between operations: 0.01 us -> 1.93 us
    pallas_call x1, Pallas kernels: 57.5 us -> 45 us  [variant(): pl.pallas_call(functools.partial(kernel, sizes, starts, halo, mid, out),...]
    slice x0 -> x1, local copies, waits for them, and re-layouts: none -> 1.33 us  [per_device(): case = jnp.where(shifts[1, 0] == 5, shifts[0, 0] - 1, shifts[1, 0] + 4)]
    unnamed x1, local copies, waits for them, and re-layouts: 1.67 us -> 0.66 us
where the time goes in v4:
time: 49.6 us; the launch traced here: 49.4 us
  Pallas kernels  45 us (91%)
  local copies, waits for them, and re-layouts  2 us (4%)
  between operations  1.93 us (4%)
    pallas_call x1, Pallas kernels, variant(): pl.pallas_call(functools.partial(kernel, sizes, starts, halo, mid, out),...  45 us
    slice x1, local copies, waits for them, and re-layouts, per_device(): case = jnp.where(shifts[1, 0] == 5, shifts[0, 0] - 1, shifts[1, 0] + 4)  1.33 us

profile of v4, /device:TPU:2, one launch (start us, length us, event | category | flops | bytes accessed | tf_op | source)
XLA Modules:
  0.0 49.4 jit_solution(8050364331667229131)
XLA Ops:
  0.0 1.3 %fusion = (s32[1,1]{1,0:T(1,128)}, s32[1,1]{1,0:T(1,128)}) fusion(s32[2,2]{1,0:T(2,128)} %param.35), kind=kLoop, calls=%fused_computation | loop fusion | bytes 16 | tf_op jit(solution)/shard_map/slice | solution.py:361
  3.3 45.5 %conditional.1 = (bf16[1,2,6,12,512]{4,1,3,2,0:T(2,128)(2,1)S(1)}) conditional(s32[]{:T(128)} %bitcast, (bf16[1,2,6,12,512]{4,1,3,2,0:T(2,128)(2,1)}, bf16[2,6,12,512]{3,0,2,1:T(2,128)(2,1)}, bf16[2,6,12,512]{3,0,2,1:T(2,128)(2,1)}, f32[512]{0:T(512)}, bf16[512,1536]{1,0:T(8,128)(2,1)}, ...), branch_computations={%region_0.1_spmd.clone, %region_1.2_spmd.clone, %region_2.3_spmd.c... | conditional | bytes 8 | solution.py:363
  3.5 45.0 %branch_6_fun.1 = bf16[72,2,512]{2,1,0:T(2,128)(2,1)S(1)} custom-call(bf16[72,2,512]{2,1,0:T(2,128)(2,1)} %bitcast.160, bf16[72,2,512]{2,1,0:T(2,128)(2,1)} %bitcast.169, bf16[72,2,512]{2,1,0:T(2,128)(2,1)} %bitcast.178, bf16[512,1536]{1,0:T(8,128)(2,1)} %get-tuple-element.415.w_qkv, bf16[512,512]{1,0:T(8,128)(2,1)} %get-tuple-element.416.w_out, ...), custom_call_target="tpu_custom_call" | custom-call | tf_op jit(solution)/shard_map/cond/branch_6_fun/pallas_call | solution.py:317
  48.7 0.7 %copy.65 = bf16[1,2,6,12,512]{4,1,3,2,0:T(2,128)(2,1)} copy(bf16[1,2,6,12,512]{4,1,3,2,0:T(2,128)(2,1)S(1)} %get-tuple-element.285) | data formatting | bytes 294912

commit v5 on v4

--- a/solution.py
+++ b/solution.py
@@ -85,7 +85,7 @@
     raw, w_qkv_v, w_out_v, land_vec_v, tables_v, shifts_v, codes_v,
     ext_halo, ext_mid, ext_out, send_halo, send_mid, send_out,
     normed_f, proj, att, cot_f, d_proj, d_mixed, direct,
-    local_sem, send_sem, recv_sem,
+    local_sem, send_sem, recv_sem, go_sem,
 ):
     n_lat, n_lon = sizes
     features = w_qkv.shape[0]
@@ -168,10 +168,13 @@
     ext_halo[0, pl.ds(0, TOK)] = raw[0].reshape(TOK, features)
     send_halo[0] = dot(pack_halo, ext_halo[0, pl.ds(0, TOK)], TN).astype(BF16)
     pl.semaphore_wait(barrier, len(to_same) + len(to_early))
-    started(halo_sends[0])
+
+    @pl.when(late)
+    def _():
+        started(halo_sends[0])
+
     ext_halo[1, pl.ds(0, TOK)] = raw[2 - step].reshape(TOK, features)
     send_halo[1] = dot(pack_halo, ext_halo[1, pl.ds(0, TOK)], TN).astype(BF16)
-    started(halo_sends[1])
 
     @pl.when(late)
     def _():
@@ -217,7 +220,18 @@
     allowed = jnp.where(seam_key == seam_query, key_valid, 0.0)
     c_vec.wait()
     c_qkv.wait()
-    arrived(halo_sends[0])
+
+    @pl.when(late)
+    def _():
+        started(halo_sends[1])
+        arrived(halo_sends[0])
+        pl.semaphore_signal(go_sem, inc=1, device_id=around(0, 0, True), device_id_type=MESH)
+
+    @pl.when(early)
+    def _():
+        pl.semaphore_wait(go_sem, 1)
+        started(halo_sends[0] + halo_sends[1])
+        arrived(halo_sends[0])
 
     lifted = dot(pick_halo, ext_halo[0]) + land * land_vec_v[...]
     centred = lifted - jnp.mean(lifted, axis=1, keepdims=True)
@@ -254,7 +268,7 @@
     for p in range(pairs):
         d_mixed[p] = d_all[:, p * 128 : (p + 1) * 128]
 
-    @pl.loop(0, pairs)
+    @pl.loop(0, pairs, unroll=2)
     def _(p):
         d_both = both_heads(d_mixed[p])
         attention = att[p]
@@ -278,6 +292,8 @@
         mid_sends[0].start()
         send_mid[...] = dot(packing(4, mid), ext_out[pl.ds(0, TOK)], TN).astype(BF16)
         started(mid_sends[1:])
+        for copy in mid_sends:
+            copy.wait_send()
 
     send_out[...] = dot(packing(5, out), ext_out[pl.ds(0, TOK)], TN).astype(BF16)
     started(out_sends)
@@ -288,11 +304,6 @@
 
     for copy in halo_sends[0] + halo_sends[1] + out_sends:
         copy.wait_send()
-
-    @pl.when(late)
-    def _():
-        for copy in mid_sends:
-            copy.wait_send()
 
 
 def variant(sizes, number, starts, states, final_cot, step_cot, w_qkv, w_out, land_vec, land_sea, ground, shifts):
@@ -343,6 +354,7 @@
             pltpu.SemaphoreType.DMA((10,)),
             pltpu.SemaphoreType.DMA((33,)),
             pltpu.SemaphoreType.DMA((33,)),
+            pltpu.SemaphoreType.REGULAR,
         ],
         compiler_params=pltpu.CompilerParams(
             collective_id=number, has_side_effects=True, vmem_limit_bytes=60 * 1024 * 1024
@@ -358,7 +370,8 @@
     others = (1, 2, 3 - WLAT, 4 - WLAT, -1)
     pairs = [(start, -1) for start in others] + [(-1, start) for start in others[:-1]]
     shifts = operands[-1]
-    case = jnp.where(shifts[1, 0] == 5, shifts[0, 0] - 1, shifts[1, 0] + 4)
+    one, five = np.array([[1, 0], [1, 0]], np.int32), np.array([[0, 0], [5, 0]], np.int32)
+    case = jnp.sum((shifts - 3) * one + jnp.minimum(5 - shifts, 1) * five)
     cases = [functools.partial(variant, sizes, number, pair) for number, pair in enumerate(pairs)]
     return lax.switch(case, cases, *operands)
 

time: 49.6 us -> 41.7 us (0.84)
  Pallas kernels: 45 us -> 38.2 us
  other arithmetic: 0 us -> 1.35 us
  local copies, waits for them, and re-layouts: 2 us -> 0.66 us
  between operations: 1.93 us -> 0.66 us
    pallas_call x1, Pallas kernels: 45 us -> 38.2 us  [variant(): pl.pallas_call(functools.partial(kernel, sizes, starts, halo, mid, out),...]
    reduce_sum x0 -> x1, other arithmetic: none -> 1.35 us  [per_device(): case = jnp.sum((shifts - 3) * one + jnp.minimum(5 - shifts, 1) * five)]
    slice x1 -> x0, local copies, waits for them, and re-layouts: 1.33 us -> none  [per_device(): case = jnp.where(shifts[1, 0] == 5, shifts[0, 0] - 1, shifts[1, 0] + 4)]
where the time goes in v5:
time: 41.7 us; the launch traced here: 41.5 us
  Pallas kernels  38.2 us (92%)
  other arithmetic  1.35 us (3%)
  local copies, waits for them, and re-layouts  0.66 us (2%)
  between operations  0.66 us (2%)
  loops' own time  0.61 us (1%)
    pallas_call x1, Pallas kernels, variant(): pl.pallas_call(functools.partial(kernel, sizes, starts, halo, mid, out),...  38.2 us
    reduce_sum x1, other arithmetic, per_device(): case = jnp.sum((shifts - 3) * one + jnp.minimum(5 - shifts, 1) * five)  1.35 us

profile of v5, /device:TPU:2, one launch (start us, length us, event | category | flops | bytes accessed | tf_op | source)
XLA Modules:
  0.0 41.5 jit_solution(17211459298119622284)
XLA Ops:
  0.0 1.4 %add_reduce_fusion = s32[]{:T(128)} fusion(s32[2,2]{1,0:T(2,128)} %constant.34.clone, s32[2,2]{1,0:T(2,128)} %param.37, s32[2,2]{1,0:T(2,128)} %constant.33.clone), kind=kLoop, calls=%fused_computation | loop fusion | flops 27 | bytes 52 | tf_op jit(solution)/shard_map/reduce_sum | solution.py:374
  2.0 38.8 %conditional.1 = (bf16[1,2,6,12,512]{4,1,3,2,0:T(2,128)(2,1)S(1)}) conditional(s32[]{:T(128)} %clamp.3, (bf16[1,2,6,12,512]{4,1,3,2,0:T(2,128)(2,1)}, bf16[2,6,12,512]{3,0,2,1:T(2,128)(2,1)}, bf16[2,6,12,512]{3,0,2,1:T(2,128)(2,1)}, f32[512]{0:T(512)}, bf16[512,1536]{1,0:T(8,128)(2,1)}, ...), branch_computations={%region_1.0_spmd.clone, %region_2.0_spmd.clone, %region_3.0_spmd.c... | conditional | bytes 8 | solution.py:376
  2.0 38.2 %branch_0_fun.1 = bf16[72,2,512]{2,1,0:T(2,128)(2,1)S(1)} custom-call(bf16[72,2,512]{2,1,0:T(2,128)(2,1)} %bitcast.153, bf16[72,2,512]{2,1,0:T(2,128)(2,1)} %bitcast.162, bf16[72,2,512]{2,1,0:T(2,128)(2,1)} %bitcast.171, bf16[512,1536]{1,0:T(8,128)(2,1)} %get-tuple-element.307.w_qkv, bf16[512,512]{1,0:T(8,128)(2,1)} %get-tuple-element.308.w_out, ...), custom_call_target="tpu_custom_call" | custom-call | tf_op jit(solution)/shard_map/cond/branch_0_fun/pallas_call | solution.py:328
  40.9 0.7 %copy.67 = bf16[1,2,6,12,512]{4,1,3,2,0:T(2,128)(2,1)} copy(bf16[1,2,6,12,512]{4,1,3,2,0:T(2,128)(2,1)S(1)} %get-tuple-element.285) | data formatting | bytes 294912

commit v6 on v5

--- a/solution.py
+++ b/solution.py
@@ -83,13 +83,14 @@
     states, final_cot, step_cot, w_qkv, w_out, land_vec, land_sea, ground, shifts, codes,
     result,
     raw, w_qkv_v, w_out_v, land_vec_v, tables_v, shifts_v, codes_v,
-    ext_halo, ext_mid, ext_out, send_halo, send_mid, send_out,
+    ext_halo, ext_mid, ext_out, send_halo, send_mid, send_out, pick_halo, pick_mid, pick_out, pack_mid, pack_out,
     normed_f, proj, att, cot_f, d_proj, d_mixed, direct,
     local_sem, send_sem, recv_sem, go_sem,
 ):
     n_lat, n_lon = sizes
     features = w_qkv.shape[0]
-    pairs = HEADS // 2
+    quads = HEADS // 4
+    wide = features // quads
     step, lat, lon = lax.axis_index("step"), lax.axis_index("lat"), lax.axis_index("lon")
     late = step == 1
     early = step == 0
@@ -103,7 +104,7 @@
 
     to_early = [(0, 0)] + [(dy, dx) for dy, dx, _, _ in mid.pieces]
     to_same = sorted(
-        {(dy, dx) for dy, dx, _, _ in halo.pieces + out.pieces} | {(-dy, -dx) for dy, dx, _, _ in halo.pieces + out.pieces}
+        {(dy * k, dx * k) for e in halo + out for dy, dx, _, _ in e.pieces for k in (1, -1)}
     )
     sign = 2 * step - 1
     barrier = pltpu.get_barrier_semaphore()
@@ -141,8 +142,8 @@
             for k, (dy, dx, offset, size) in enumerate(exchange.pieces)
         ]
 
-    halo_sends = [remotes(8 * i, halo, send_halo.at[i], ext_halo.at[i]) for i in range(2)]
-    out_sends = remotes(16, out, send_out, ext_out)
+    halo_sends = [[remotes(8 * i, halo[half], send_halo.at[i], ext_halo.at[i]) for i in range(2)] for half in range(2)]
+    out_sends = [remotes(16, out[half], send_out, ext_out) for half in range(2)]
     mid_sends = [pltpu.make_async_remote_copy(
         src_ref=ext_out.at[pl.ds(0, TOK)], dst_ref=ext_mid.at[pl.ds(0, TOK)],
         send_sem=send_sem.at[32], recv_sem=recv_sem.at[32], device_id=around(0, 0, True), device_id_type=MESH,
@@ -156,40 +157,59 @@
         for copy in copies:
             copy.wait_recv()
 
-    def packing(row, exchange):
-        token = lax.broadcasted_iota(jnp.int32, (TOK, exchange.sent), 0)
-        return one_hot(token, codes_v[row : row + 1, : exchange.sent])
+    def own_row(first, width):
+        return jnp.where(late, codes_v[first + 1 : first + 2, :width], codes_v[first : first + 1, :width])
+
+    def packing(row):
+        token = lax.broadcasted_iota(jnp.int32, (TOK, row.shape[1]), 0)
+        same = lax.broadcasted_iota(jnp.int32, (TOK, TOK), 0) == lax.broadcasted_iota(jnp.int32, (TOK, TOK), 1)
+        return dot(one_hot(token, row), jnp.where(same, 1.0, 0.0).astype(BF16), TN).astype(BF16)
+
+    def clear(target, exchange):
+        rows = target.shape[0] - exchange.held
+        if rows:
+            target[pl.ds(exchange.held, rows)] = jnp.zeros((rows, features), BF16)
 
     c_codes.wait()
-    pack_halo = packing(3, halo)
+    pack_halo = packing(own_row(8, send_halo.shape[1]))
     c_state.wait()
     c_step.wait()
     c_final.wait()
     ext_halo[0, pl.ds(0, TOK)] = raw[0].reshape(TOK, features)
-    send_halo[0] = dot(pack_halo, ext_halo[0, pl.ds(0, TOK)], TN).astype(BF16)
+    send_halo[0] = dot(pack_halo, ext_halo[0, pl.ds(0, TOK)]).astype(BF16)
     pl.semaphore_wait(barrier, len(to_same) + len(to_early))
 
     @pl.when(late)
     def _():
-        started(halo_sends[0])
+        started(halo_sends[1][0])
 
     ext_halo[1, pl.ds(0, TOK)] = raw[2 - step].reshape(TOK, features)
-    send_halo[1] = dot(pack_halo, ext_halo[1, pl.ds(0, TOK)], TN).astype(BF16)
+    send_halo[1] = dot(pack_halo, ext_halo[1, pl.ds(0, TOK)]).astype(BF16)
 
     @pl.when(late)
     def _():
         direct[...] = raw[2].reshape(TOK, features)
+        clear(ext_halo.at[0], halo[1])
+        clear(ext_halo.at[1], halo[1])
+        clear(ext_out, out[1])
 
     @pl.when(early)
     def _():
         direct[...] = jnp.zeros((TOK, features), BF16)
+        clear(ext_halo.at[0], halo[0])
+        clear(ext_halo.at[1], halo[0])
+        clear(ext_out, out[0])
 
     c_shift.wait()
     s_early, s_late = starts
     t_early, t_late = (jnp.where(b >= 6, b - WLON, b) for b in (shifts_v[0, 1], shifts_v[1, 1]))
     s = jnp.where(late, s_late, s_early)
     t = jnp.where(late, t_late, t_early)
-    pick_halo = one_hot(read_codes(s, t), codes_v[0:1, : halo.held])
+    pick_halo[...] = one_hot(read_codes(s, t), own_row(0, ext_halo.shape[1]))
+    pick_out[...] = one_hot(read_codes(-s, -t), own_row(3, ext_out.shape[0]))
+    pack_out[...] = packing(own_row(11, send_out.shape[0]))
+    pack_mid[...] = packing(codes_v[10:11, : mid.sent])
+    pick_mid[...] = one_hot(read_codes(s_early - s_late, t_early - t_late), codes_v[2:3, : mid.held])
 
     row, col, level = frame_places()
     lat_total, lon_total = tables_v.shape[1], tables_v.shape[2]
@@ -213,7 +233,8 @@
     shift_lat = jnp.where(s < 0, s + WLAT, s)
     window = jnp.where(s < 0, lax.rem(lat + (n_lat - 1), n_lat), lat)
     first_seam = jnp.where(window == n_lat - 1, WLAT - shift_lat, WLAT)
-    lane = lax.broadcasted_iota(jnp.int32, (1, 2 * TOK), 1)
+    lane = lax.broadcasted_iota(jnp.int32, (1, 4 * TOK), 1)
+    lane = jnp.where(lane >= 2 * TOK, lane - 2 * TOK, lane)
     lane = jnp.where(lane >= TOK, lane - TOK, lane)
     seam_key = jnp.where(row >= first_seam, 1, 0)
     seam_query = jnp.where(quotient(lane >> 1, WLON) >= first_seam, 1, 0)
@@ -223,64 +244,72 @@
 
     @pl.when(late)
     def _():
-        started(halo_sends[1])
-        arrived(halo_sends[0])
+        started(halo_sends[1][1])
+        arrived(halo_sends[1][0])
         pl.semaphore_signal(go_sem, inc=1, device_id=around(0, 0, True), device_id_type=MESH)
 
     @pl.when(early)
     def _():
         pl.semaphore_wait(go_sem, 1)
-        started(halo_sends[0] + halo_sends[1])
-        arrived(halo_sends[0])
-
-    lifted = dot(pick_halo, ext_halo[0]) + land * land_vec_v[...]
+        started(halo_sends[0][0] + halo_sends[0][1])
+        arrived(halo_sends[0][0])
+
+    lifted = dot(pick_halo[...], ext_halo[0]) + land * land_vec_v[...]
     centred = lifted - jnp.mean(lifted, axis=1, keepdims=True)
     scale = lax.rsqrt(jnp.mean(centred * centred, axis=1, keepdims=True) + 1e-05)
     normed = centred * scale
     normed_f[...] = normed
     projected = dot(normed.astype(BF16), w_qkv_v[...]).astype(BF16)
-    for p in range(3 * pairs):
-        proj[p] = projected[:, p * 128 : (p + 1) * 128]
-    half = lax.broadcasted_iota(jnp.int32, (TOK, 128), 1) < 64
-    zero = jnp.zeros((TOK, 128), BF16)
-
-    def both_heads(pair):
-        return jnp.concatenate([jnp.where(half, pair, zero), jnp.where(half, zero, pair)], axis=0)
-
-    @pl.loop(0, pairs)
+    for p in range(3 * quads):
+        proj[p] = projected[:, p * wide : (p + 1) * wide]
+    group = lax.broadcasted_iota(jnp.int32, (TOK, wide), 1) >> 6
+    zero = jnp.zeros((TOK, wide), BF16)
+
+    def by_head(quad):
+        return jnp.concatenate([jnp.where(group == h, quad, zero) for h in range(4)], axis=0)
+
+    @pl.loop(0, quads)
     def _(p):
-        weights = jnp.exp(dot(proj[pairs + p], both_heads(proj[p] * 0.125), NT)) * allowed
+        weights = jnp.exp(dot(proj[quads + p], by_head(proj[p] * 0.125), NT)) * allowed
         att[p] = weights * (1.0 / jnp.sum(weights, axis=0, keepdims=True))
 
-    arrived(halo_sends[1])
-    cot_f[...] = dot(pick_halo, ext_halo[1])
+    @pl.when(late)
+    def _():
+        arrived(halo_sends[1][1])
+
+    @pl.when(early)
+    def _():
+        arrived(halo_sends[0][1])
+
+    cot_f[...] = dot(pick_halo[...], ext_halo[1])
     c_out.wait()
 
     @pl.when(early)
     def _():
-        pick = one_hot(read_codes(s_early - s_late, t_early - t_late), codes_v[1:2, : mid.held])
         arrived(mid_sends)
-        cot_f[...] += dot(pick, ext_mid[...])
+        cot_f[...] += dot(pick_mid[...], ext_mid[...])
 
     cot_w = cot_f[...].astype(BF16)
 
     d_all = dot(cot_w, w_out_v[...], NT).astype(BF16)
-    for p in range(pairs):
-        d_mixed[p] = d_all[:, p * 128 : (p + 1) * 128]
-
-    @pl.loop(0, pairs, unroll=2)
+    for p in range(quads):
+        d_mixed[p] = d_all[:, p * wide : (p + 1) * wide]
+
+    @pl.loop(0, quads)
     def _(p):
-        d_both = both_heads(d_mixed[p])
+        d_heads = by_head(d_mixed[p])
         attention = att[p]
-        inner = attention * dot(proj[2 * pairs + p], d_both, NT)
+        inner = attention * dot(proj[2 * quads + p], d_heads, NT)
         d_scores = (inner - attention * jnp.sum(inner, axis=0, keepdims=True)).astype(BF16)
-        d_query = dot(d_scores, proj[pairs + p], TN)
-        d_query = jnp.where(half, d_query[:TOK], d_query[TOK:]) * 0.125
-        d_proj[p] = d_query.astype(BF16)
-        d_proj[pairs + p] = dot(d_scores, both_heads(proj[p] * 0.125)).astype(BF16)
-        d_proj[2 * pairs + p] = dot(attention.astype(BF16), d_both).astype(BF16)
-
-    d_all = jnp.concatenate([d_proj[p] for p in range(3 * pairs)], axis=1)
+        d_each = dot(d_scores, proj[quads + p], TN)
+        d_query = d_each[:TOK]
+        for h in range(1, 4):
+            d_query = jnp.where(group == h, d_each[h * TOK : (h + 1) * TOK], d_query)
+        d_proj[p] = (d_query * 0.125).astype(BF16)
+        d_proj[quads + p] = dot(d_scores, by_head(proj[p] * 0.125)).astype(BF16)
+        d_proj[2 * quads + p] = dot(attention.astype(BF16), d_heads).astype(BF16)
+
+    d_all = jnp.concatenate([d_proj[p] for p in range(3 * quads)], axis=1)
     d_normed = dot(d_all, w_qkv_v[...], NT).astype(BF16).astype(F32)
     normed = normed_f[...]
     along = jnp.mean(d_normed * normed, axis=1, keepdims=True)
@@ -290,33 +319,50 @@
     @pl.when(late)
     def _():
         mid_sends[0].start()
-        send_mid[...] = dot(packing(4, mid), ext_out[pl.ds(0, TOK)], TN).astype(BF16)
+        send_mid[...] = dot(pack_mid[...], ext_out[pl.ds(0, TOK)]).astype(BF16)
         started(mid_sends[1:])
         for copy in mid_sends:
             copy.wait_send()
 
-    send_out[...] = dot(packing(5, out), ext_out[pl.ds(0, TOK)], TN).astype(BF16)
-    started(out_sends)
-    pick_out = one_hot(read_codes(-s, -t), codes_v[2:3, : out.held])
-    arrived(out_sends)
-    home = dot(pick_out, ext_out[...]) + direct[...].astype(F32)
+    send_out[...] = dot(pack_out[...], ext_out[pl.ds(0, TOK)]).astype(BF16)
+
+    @pl.when(late)
+    def _():
+        started(out_sends[1])
+        arrived(out_sends[1])
+
+    @pl.when(early)
+    def _():
+        started(out_sends[0])
+        arrived(out_sends[0])
+
+    home = dot(pick_out[...], ext_out[...]) + direct[...].astype(F32)
     result[...] = home.astype(BF16).reshape(result.shape)
 
-    for copy in halo_sends[0] + halo_sends[1] + out_sends:
-        copy.wait_send()
+    @pl.when(late)
+    def _():
+        for copy in halo_sends[1][0] + halo_sends[1][1] + out_sends[1]:
+            copy.wait_send()
+
+    @pl.when(early)
+    def _():
+        for copy in halo_sends[0][0] + halo_sends[0][1] + out_sends[0]:
+            copy.wait_send()
 
 
 def variant(sizes, number, starts, states, final_cot, step_cot, w_qkv, w_out, land_vec, land_sea, ground, shifts):
-    before, after = max(-min(starts), 0), max(max(starts), 0)
+    before, after = [max(-start, 0) for start in starts], [max(start, 0) for start in starts]
     apart = starts[0] - starts[1]
-    halo = Exchange(after, before, 5, 6)
+    halo = [Exchange(after[half], before[half], 5, 6) for half in range(2)]
     mid = Exchange(max(apart, 0), max(-apart, 0), 6, 6)
-    out = Exchange(before, after, 6, 5)
+    out = [Exchange(before[half], after[half], 6, 5) for half in range(2)]
     features = w_qkv.shape[0]
-    codes = np.full((8, 512), -1, np.int32)
-    for i, e in enumerate((halo, mid, out)):
+    codes = np.full((16, 512), -1, np.int32)
+    for i, e in enumerate(halo + [mid] + out):
         codes[i, : e.held] = e.codes
-        codes[3 + i, : e.sent] = e.packed
+        codes[8 + i, : e.sent] = e.packed
+    halo_held, halo_sent = max(e.held for e in halo), max(e.sent for e in halo)
+    out_held, out_sent = max(e.held for e in out), max(e.sent for e in out)
     held_spec = pl.BlockSpec(memory_space=pltpu.HBM)
 
     def field(*shape):
@@ -338,18 +384,23 @@
             pltpu.VMEM((2,) + land_sea.shape, jnp.int32),
             pltpu.SMEM(shifts.shape, jnp.int32),
             pltpu.VMEM(codes.shape, jnp.int32),
-            field(2, halo.held, features),
+            field(2, halo_held, features),
             field(mid.held, features),
-            field(out.held, features),
-            field(2, halo.sent, features),
+            field(out_held, features),
+            field(2, halo_sent, features),
             field(mid.sent, features),
-            field(out.sent, features),
+            field(out_sent, features),
+            field(TOK, halo_held),
+            field(TOK, mid.held),
+            field(TOK, out_held),
+            field(mid.sent, TOK),
+            field(out_sent, TOK),
             pltpu.VMEM((TOK, features), F32),
-            field(3 * HEADS // 2, TOK, 128),
-            pltpu.VMEM((HEADS // 2, TOK, 2 * TOK), F32),
+            field(3 * HEADS // 4, TOK, 4 * features // HEADS),
+            pltpu.VMEM((HEADS // 4, TOK, 4 * TOK), F32),
             pltpu.VMEM((TOK, features), F32),
-            field(3 * HEADS // 2, TOK, 128),
-            field(HEADS // 2, TOK, 128),
+            field(3 * HEADS // 4, TOK, 4 * features // HEADS),
+            field(HEADS // 4, TOK, 4 * features // HEADS),
             field(TOK, features),
             pltpu.SemaphoreType.DMA((10,)),
             pltpu.SemaphoreType.DMA((33,)),

time: 41.7 us -> 38.1 us (0.914); the launches traced: 41.5 us -> 38.5 us
  Pallas kernels: 38.2 us -> 35 us
    pallas_call x1, Pallas kernels: 38.2 us -> 35 us  [variant(): pl.pallas_call(functools.partial(kernel, sizes, starts, halo, mid, out),...]
where the time goes in v6:
time: 38.1 us; the launch traced here: 38.5 us
  Pallas kernels  35 us (92%)
  other arithmetic  1.35 us (4%)
  loops' own time  0.84 us (2%)
  local copies, waits for them, and re-layouts  0.66 us (2%)
  between operations  0.66 us (2%)
    pallas_call x1, Pallas kernels, variant(): pl.pallas_call(functools.partial(kernel, sizes, starts, halo, mid, out),...  35 us
    reduce_sum x1, other arithmetic, per_device(): case = jnp.sum((shifts - 3) * one + jnp.minimum(5 - shifts, 1) * five)  1.35 us
    another operation x1, loops' own time, per_device(): return lax.switch(case, cases, *operands)  0.84 us

profile of v6, /device:TPU:2, one launch (start us, length us, event | category | flops | bytes accessed | tf_op | source)
XLA Modules:
  0.0 38.5 jit_solution(485587144498425254)
XLA Ops:
  0.0 1.4 %add_reduce_fusion = s32[]{:T(128)} fusion(s32[2,2]{1,0:T(2,128)} %constant.34.clone, s32[2,2]{1,0:T(2,128)} %param.37, s32[2,2]{1,0:T(2,128)} %constant.33.clone), kind=kLoop, calls=%fused_computation | loop fusion | flops 27 | bytes 52 | tf_op jit(solution)/shard_map/reduce_sum | solution.py:425
  2.0 35.8 %conditional.1 = (bf16[1,2,6,12,512]{4,1,3,2,0:T(2,128)(2,1)S(1)}) conditional(s32[]{:T(128)} %clamp.3, (bf16[1,2,6,12,512]{4,1,3,2,0:T(2,128)(2,1)}, bf16[2,6,12,512]{3,0,2,1:T(2,128)(2,1)}, bf16[2,6,12,512]{3,0,2,1:T(2,128)(2,1)}, f32[512]{0:T(512)}, bf16[512,1536]{1,0:T(8,128)(2,1)}, ...), branch_computations={%region_1.0_spmd.clone, %region_2.0_spmd.clone, %region_3.0_spmd.c... | conditional | bytes 8 | solution.py:427
  2.5 35.0 %branch_8_fun.1 = bf16[72,2,512]{2,1,0:T(2,128)(2,1)S(1)} custom-call(bf16[72,2,512]{2,1,0:T(2,128)(2,1)} %bitcast.161, bf16[72,2,512]{2,1,0:T(2,128)(2,1)} %bitcast.170, bf16[72,2,512]{2,1,0:T(2,128)(2,1)} %bitcast.179, bf16[512,1536]{1,0:T(8,128)(2,1)} %get-tuple-element.451.w_qkv, bf16[512,512]{1,0:T(8,128)(2,1)} %get-tuple-element.452.w_out, ...), custom_call_target="tpu_custom_call" | custom-call | tf_op jit(solution)/shard_map/cond/branch_8_fun/pallas_call | solution.py:374
  37.8 0.7 %copy.67 = bf16[1,2,6,12,512]{4,1,3,2,0:T(2,128)(2,1)} copy(bf16[1,2,6,12,512]{4,1,3,2,0:T(2,128)(2,1)S(1)} %get-tuple-element.285) | data formatting | bytes 294912
